TPU v7x, 128 devices: a whole 4x4x4 slice. The times are simulated.
128 devices in a mesh: clip: 16 (over y, z), tm: 4 (over x_hi, core), rows: 2 (over x_lo).
Axes of the slice: x: 4 (x_hi: 2, x_lo: 2; x = x_hi * 2 + x_lo), y: 4, z: 4, core: 2. Of those that a mesh axis runs over, the one named last changes fastest.
Arguments:
- inputs: bfloat16 [16, 8, 2, 128, 384], P('clip', 'tm', 'rows'), may hold values from -40 to 40
- cotangent: bfloat16 [16, 8, 2, 128, 384], P('clip', 'tm', 'rows'), may hold values from -6 to 6
- weight: bfloat16 [10368, 384], replicated, may hold values from -0.0625 to 0.0625
- gain: float32 [384], replicated, may hold values from 0.5 to 1.5
- shift_term: float32 [384], replicated, may hold values from -3 to 3
Outputs:
- input_grad: bfloat16 [16, 8, 2, 128, 384], P('clip', 'tm', 'rows')
- weight_grad: float32 [10368, 384], P(('clip', 'tm', 'rows'))
All inputs are finite; a program needn't handle non-finite values.
Results may differ from a plain program's by a relative error of at most 0.0004.
The roundings to bfloat16 on the way count: a program that leaves them out, or rounds other values in their place, can miss the bound.
Values may be sent and summed in bfloat16 or wider, within the bound.
A program may use at most 128 MiB of HBM per device.

v0:
```python
import jax
import jax.numpy as jnp
from jax import lax
from jax.sharding import PartitionSpec as P

GROUPS = 32


EPSILON = 1e-05


def from_behind(block, axis, distance):
    devices = range(lax.axis_size(axis))
    route = [(i - distance, i) for i in devices if i - distance in devices]
    return lax.ppermute(block, axis, route)


def with_halo(value, sides, width):
    for axis, dim in sides:
        size, length = (lax.axis_size(axis), value.shape[dim])
        up = [(i, (i + 1) % size) for i in range(size - 1)]
        down = [(j, i) for i, j in up]
        last = lax.slice_in_dim(value, length - width, length, axis=dim)
        first = lax.slice_in_dim(value, 0, width, axis=dim)
        before = lax.ppermute(last, axis, up)
        after = lax.ppermute(first, axis, down)
        value = jnp.concatenate([before, value, after], axis=dim)
    return value


def group_totals(values):
    channels = values.shape[-1]
    return jnp.sum(values.reshape(-1, GROUPS, channels // GROUPS), axis=(0, 2))


def spread_groups(stats, channels):
    return jnp.repeat(stats, channels // GROUPS)


def make_patches(padded, frames, bands, columns, channels, mirrored):
    blocks = []
    for tap_t in range(3):
        for tap_h in range(3):
            for tap_w in range(3):
                if mirrored:
                    off_t, off_h, off_w = (2 - tap_t, 2 - tap_h, 2 - tap_w)
                else:
                    off_t, off_h, off_w = (tap_t, tap_h, tap_w)
                window = padded[
                    off_t : off_t + frames, off_h : off_h + bands, off_w : off_w + columns
                ]
                blocks.append(window.reshape(-1, channels))
    return jnp.concatenate(blocks, 1)


def per_device(inputs, cotangent, weight, gain, shift_term):
    signal = inputs[0]
    upstream = cotangent[0]
    frames, bands, columns, channels = signal.shape
    band_devices = lax.axis_size("tm") * lax.axis_size("rows")
    cells_group = frames * bands * columns * band_devices * (channels // GROUPS)
    values = signal.astype(jnp.float32)
    sum_group, square_group = lax.psum(
        (group_totals(values), group_totals(values * values)), ("tm", "rows")
    )
    mean_group = sum_group / cells_group
    rstd_group = lax.rsqrt(square_group / cells_group - mean_group * mean_group + EPSILON)
    mean_chan = spread_groups(mean_group, channels)
    rstd_chan = spread_groups(rstd_group, channels)
    normed_block = (signal.astype(jnp.float32) - mean_chan) * rstd_chan
    shifted = normed_block * gain + shift_term
    active = jax.nn.silu(shifted).astype(jnp.bfloat16)
    earlier = from_behind(active, "tm", 1)
    extended = jnp.concatenate([earlier, active], 0)
    act_band = with_halo(extended, (("rows", 1),), 1)
    act_full = jnp.pad(act_band, ((0, 0), (0, 0), (1, 1), (0, 0)))
    later = from_behind(upstream, "tm", -1)
    cot_ext = jnp.concatenate([upstream, later], 0)
    cot_band = with_halo(cot_ext, (("rows", 1),), 1)
    cot_full = jnp.pad(cot_band, ((0, 0), (0, 0), (1, 1), (0, 0)))
    act_patch = make_patches(act_full, frames, bands, columns, channels, False)
    cot_patch = make_patches(cot_full, frames, bands, columns, channels, True)
    cot_rows = upstream.reshape(-1, channels)
    kernel_cube = weight.reshape(-1, channels, channels)
    grad_active = jnp.einsum(
        "ntk,tck->nc",
        cot_patch.reshape(-1, kernel_cube.shape[0], channels),
        kernel_cube,
        preferred_element_type=jnp.float32,
    )
    grad_active = grad_active.reshape(frames, bands, columns, channels)
    sigma = jax.nn.sigmoid(shifted)
    grad_normed = grad_active * sigma * (1.0 + shifted * (1.0 - sigma)) * gain
    first_sum, second_sum = lax.psum(
        (group_totals(grad_normed), group_totals(grad_normed * normed_block)), ("tm", "rows")
    )
    first_mean = spread_groups(first_sum / cells_group, channels)
    second_mean = spread_groups(second_sum / cells_group, channels)
    input_grad = upstream.astype(jnp.float32) + rstd_chan * (
        grad_normed - first_mean - normed_block * second_mean
    )
    summed = lax.psum_scatter(
        lax.dot_general(
            act_patch, cot_rows, (((0,), (0,)), ((), ())), preferred_element_type=jnp.float32
        ),
        ("clip", "tm", "rows"),
        scatter_dimension=0,
        tiled=True,
    )
    grad_scale = 1.0 / (lax.axis_size("clip") * frames * lax.axis_size("tm"))
    return (input_grad.astype(jnp.bfloat16)[None], summed * grad_scale)


def solution(mesh):
    return jax.shard_map(
        per_device,
        mesh=mesh,
        in_specs=(
            P("clip", "tm", "rows", None, None),
            P("clip", "tm", "rows", None, None),
            P(),
            P(),
            P(),
        ),
        out_specs=(P("clip", "tm", "rows", None, None), P(("clip", "tm", "rows"), None)),
        check_vma=False,
    )
```

profile of v0, /device:TPU:1, one launch (start us, length us, event | category | flops | bytes accessed | tf_op | source)
XLA Modules:
  0.0 528.2 jit_solution(4164161112369092851)
XLA Ops:
  2.1 15.4 %all-reduce.5 = (f32[32]{0:T(128)S(1)}, f32[32]{0:T(128)S(1)}) all-reduce(f32[32]{0:T(128)S(1)} %reduce_sum.54, f32[32]{0:T(128)S(1)} %reduce_sum.51), channel_id=1, replica_groups=mesh['clip'=16,'tm'=4,'rows'=2] {'tm','rows'}, use_global_device_ids=true, to_apply=%region_5.6 | all-reduce | flops 64 | bytes 512 | tf_op jit(solution)/shard_map/psum | solution.py:63
  18.9 2.8 collective-permute-start.3
  21.7 1.9 collective-permute-start
  25.1 2.7 collective-permute-start.4
  27.9 1.3 collective-permute-start.5
  29.2 2.7 collective-permute-done
  32.8 1.4 collective-permute-start.1
  34.2 1.3 collective-permute-start.2
  36.5 3.9 collective-permute-done.5
  42.9 7.1 %fusion.26 = f32[10368,384]{1,0:T(8,128)} fusion(bf16[256,10368]{1,0:T(8,128)(2,1)S(1)} %constant_dynamic-update-slice_fusion.27, bf16[256,384]{1,0:T(8,128)(2,1)S(1)} %bitcast.127), kind=kOutput, calls=%fused_computation.107 | convolution fusion | flops 2038431744 | bytes 21430272 | tf_op jit(solution)/shard_map/dot_general | solution.py:103
  50.0 361.1 %fusion = f32[96,384]{1,0:T(8,128)S(1)} fusion(f32[10368,384]{1,0:T(8,128)} %fusion.26), kind=kCustom, calls=%all-reduce-scatter | all-reduce-scatter fusion | flops 4718593 | bytes 16072704
  411.1 1.3 collective-permute-start.10
  412.4 1.3 collective-permute-start.11
  413.7 1.9 collective-permute-start.12
  415.6 2.0 collective-permute-start.13
  423.4 10.7 %collective-permute-start.15 = (f32[96,384]{1,0:T(8,128)S(1)}, f32[96,384]{1,0:T(8,128)S(1)}, u32[]{:S(2)}, u32[]{:S(2)}) collective-permute-start(f32[96,384]{1,0:T(8,128)S(1)} %fusion), channel_id=1, source_target_pairs={{0,10},{1,11},{2,12},{3,13},{4,14},{5,15},{6,16},{7,17},{8,18},{9,... | collective-permute-start | bytes 442376
  434.1 1.3 collective-permute-start.16
  435.4 1.3 collective-permute-start.17
  436.7 1.3 collective-permute-start.18
  438.1 3.0 fusion.19
  441.6 17.3 %all-reduce.4 = (f32[32]{0:T(128)S(1)}, f32[32]{0:T(128)S(1)}) all-reduce(f32[32]{0:T(128)S(1)} %reduce_sum.75, f32[32]{0:T(128)S(1)} %reduce_sum.72), channel_id=1, replica_groups=mesh['clip'=16,'tm'=4,'rows'=2] {'tm','rows'}, use_global_device_ids=true, to_apply=%region_11.12 | all-reduce | flops 64 | bytes 512 | tf_op jit(solution)/shard_map/psum | solution.py:94
  458.9 8.1 %collective-permute-start.19 = (f32[96,384]{1,0:T(8,128)S(1)}, f32[96,384]{1,0:T(8,128)S(1)}, u32[]{:S(2)}, u32[]{:S(2)}) collective-permute-start(f32[96,384]{1,0:T(8,128)S(1)} %fusion), channel_id=1, source_target_pairs={{0,14},{1,15},{2,16},{3,17},{4,18},{5,19},{6,20},{7,21},{8,22},{9,... | collective-permute-start | bytes 442376
  467.0 9.4 %collective-permute-start.20 = (f32[96,384]{1,0:T(8,128)S(1)}, f32[96,384]{1,0:T(8,128)S(1)}, u32[]{:S(2)}, u32[]{:S(2)}) collective-permute-start(f32[96,384]{1,0:T(8,128)S(1)} %fusion), channel_id=1, source_target_pairs={{0,15},{1,16},{2,17},{3,18},{4,19},{5,20},{6,21},{7,22},{8,23},{9,... | collective-permute-start | bytes 442376
  476.4 9.2 %collective-permute-start.21 = (f32[96,384]{1,0:T(8,128)S(1)}, f32[96,384]{1,0:T(8,128)S(1)}, u32[]{:S(2)}, u32[]{:S(2)}) collective-permute-start(f32[96,384]{1,0:T(8,128)S(1)} %fusion), channel_id=1, source_target_pairs={{0,16},{1,17},{2,18},{3,19},{4,20},{5,21},{6,22},{7,23},{8,24},{9,... | collective-permute-start | bytes 442376
  485.7 2.5 collective-permute-start.22
  488.2 4.5 collective-permute-start.23
  493.2 1.3 collective-permute-start.24
  494.5 1.9 collective-permute-start.6
  496.4 4.5 collective-permute-start.7
  501.0 2.1 collective-permute-start.8
  503.1 3.3 collective-permute-start.9
  508.7 18.8 %concatenate.106 = f32[2001,384]{1,0:T(8,128)S(1)} concatenate(f32[81,384]{1,0:T(8,128)} %copy-done.20, f32[96,384]{1,0:T(8,128)} %copy-done.16, f32[96,384]{1,0:T(8,128)} %copy-done.15, f32[96,384]{1,0:T(8,128)} %copy-done.14, f32[96,384]{1,0:T(8,128)} %copy-done.13, f32[96,384]{1,0:T(8,128)} %copy-done.12, f32[96,384]{1,0:T(8,128)} %copy-done.11, f32[96,384]{1,0:T(8,128)} %copy-done.10, ...), dimensions={0} | concatenate | bytes 6147072
  (166 shorter events, 17.7 us)
Async XLA Ops:
  18.9 5.4 %collective-permute-start.3 = (bf16[2,1,128,384]{3,2,0,1:T(8,128)(2,1)S(1)}, bf16[2,1,128,384]{3,2,0,1:T(8,128)(2,1)S(1)}, u32[]{:S(2)}, u32[]{:S(2)}) collective-permute-start(bf16[2,1,128,384]{3,2,0,1:T(8,128)(2,1)S(1)} %multiply_convert_fusion.1), channel_id=1, source_target_pairs={{0,2},{2,4},{4,6},{1,3},{3,5},{5,7},{8,10},{10,12},{12,14},{9,11},... | collective-permute-start | bytes 589832 | tf_op jit(solution)/shard_map/ppermute | solution.py:15
  21.7 10.1 %collective-permute-start = (bf16[2,1,128,384]{3,2,0,1:T(8,128)(2,1)}, bf16[2,1,128,384]{3,2,0,1:T(8,128)(2,1)S(1)}, u32[]{:S(2)}, u32[]{:S(2)}) collective-permute-start(bf16[2,1,128,384]{3,2,0,1:T(8,128)(2,1)} %bitcast.124), channel_id=1, source_target_pairs={{2,0},{4,2},{6,4},{3,1},{5,3},{7,5},{10,8},{12,10},{14,12},{11,9},... | collective-permute-start | bytes 589832 | tf_op jit(solution)/shard_map/ppermute | solution.py:15
  25.1 11.3 %collective-permute-start.4 = (bf16[4,1,128,384]{3,2,0,1:T(8,128)(2,1)}, bf16[4,1,128,384]{3,2,0,1:T(8,128)(2,1)S(1)}, u32[]{:S(2)}, u32[]{:S(2)}) collective-permute-start(bf16[4,1,128,384]{3,2,0,1:T(8,128)(2,1)} %pad_maximum_fusion.1), channel_id=1, source_target_pairs={{0,1},{2,3},{4,5},{6,7},{8,9},{10,11},{12,13},{14,15},{16,17},{18,... | collective-permute-start | bytes 1179656 | tf_op jit(solution)/shard_map/ppermute | solution.py:25
  27.9 12.5 %collective-permute-start.5 = (bf16[4,1,128,384]{3,2,0,1:T(8,128)(2,1)}, bf16[4,1,128,384]{3,2,0,1:T(8,128)(2,1)S(1)}, u32[]{:S(2)}, u32[]{:S(2)}) collective-permute-start(bf16[4,1,128,384]{3,2,0,1:T(8,128)(2,1)} %pad_maximum_fusion.1), channel_id=1, source_target_pairs={{1,0},{3,2},{5,4},{7,6},{9,8},{11,10},{13,12},{15,14},{17,16},{19,... | collective-permute-start | bytes 1179656 | tf_op jit(solution)/shard_map/ppermute | solution.py:26
  32.8 382.8 %collective-permute-start.1 = (bf16[4,1,128,384]{3,2,0,1:T(8,128)(2,1)S(1)}, bf16[4,1,128,384]{3,2,0,1:T(8,128)(2,1)S(1)}, u32[]{:S(2)}, u32[]{:S(2)}) collective-permute-start(bf16[4,1,128,384]{3,2,0,1:T(8,128)(2,1)S(1)} %pad_maximum_fusion), channel_id=1, source_target_pairs={{0,1},{2,3},{4,5},{6,7},{8,9},{10,11},{12,13},{14,15},{16,17},{18,... | collective-permute-start | bytes 1179656 | tf_op jit(solution)/shard_map/ppermute | solution.py:25
  34.2 383.4 %collective-permute-start.2 = (bf16[4,1,128,384]{3,2,0,1:T(8,128)(2,1)S(1)}, bf16[4,1,128,384]{3,2,0,1:T(8,128)(2,1)S(1)}, u32[]{:S(2)}, u32[]{:S(2)}) collective-permute-start(bf16[4,1,128,384]{3,2,0,1:T(8,128)(2,1)S(1)} %pad_maximum_fusion), channel_id=1, source_target_pairs={{1,0},{3,2},{5,4},{7,6},{9,8},{11,10},{13,12},{15,14},{17,16},{19,... | collective-permute-start | bytes 1179656 | tf_op jit(solution)/shard_map/ppermute | solution.py:26
  411.1 12.3 %collective-permute-start.10 = (f32[96,384]{1,0:T(8,128)S(1)}, f32[96,384]{1,0:T(8,128)S(1)}, u32[]{:S(2)}, u32[]{:S(2)}) collective-permute-start(f32[96,384]{1,0:T(8,128)S(1)} %fusion), channel_id=1, source_target_pairs={{0,5},{1,6},{2,7},{3,8},{4,9},{5,10},{6,11},{7,12},{8,13},{9,14},{... | collective-permute-start | bytes 442376
  412.4 21.7 %collective-permute-start.11 = (f32[96,384]{1,0:T(8,128)S(1)}, f32[96,384]{1,0:T(8,128)S(1)}, u32[]{:S(2)}, u32[]{:S(2)}) collective-permute-start(f32[96,384]{1,0:T(8,128)S(1)} %fusion), channel_id=1, source_target_pairs={{0,6},{1,7},{2,8},{3,9},{4,10},{5,11},{6,12},{7,13},{8,14},{9,15},... | collective-permute-start | bytes 442376
  413.7 21.7 %collective-permute-start.12 = (f32[96,384]{1,0:T(8,128)S(1)}, f32[96,384]{1,0:T(8,128)}, u32[]{:S(2)}, u32[]{:S(2)}) collective-permute-start(f32[96,384]{1,0:T(8,128)S(1)} %fusion), channel_id=1, source_target_pairs={{0,7},{1,8},{2,9},{3,10},{4,11},{5,12},{6,13},{7,14},{8,15},{9,16}... | collective-permute-start | bytes 442376
  415.6 21.1 %collective-permute-start.13 = (f32[96,384]{1,0:T(8,128)S(1)}, f32[96,384]{1,0:T(8,128)}, u32[]{:S(2)}, u32[]{:S(2)}) collective-permute-start(f32[96,384]{1,0:T(8,128)S(1)} %fusion), channel_id=1, source_target_pairs={{0,8},{1,9},{2,10},{3,11},{4,12},{5,13},{6,14},{7,15},{8,16},{9,17... | collective-permute-start | bytes 442376
  417.6 4.5 collective-permute-start.25
  422.1 85.1 %copy-start.20 = (f32[81,384]{1,0:T(8,128)}, f32[81,384]{1,0:T(8,128)S(1)}, u32[]{:S(2)}) copy-start(f32[81,384]{1,0:T(8,128)S(1)} %collective-permute-done.25) | copy-start | bytes 373252
  422.1 36.8 %collective-permute-start.14 = (f32[96,384]{1,0:T(8,128)S(1)}, f32[96,384]{1,0:T(8,128)S(1)}, u32[]{:S(2)}, u32[]{:S(2)}) collective-permute-start(f32[96,384]{1,0:T(8,128)S(1)} %fusion), channel_id=1, source_target_pairs={{0,9},{1,10},{2,11},{3,12},{4,13},{5,14},{6,15},{7,16},{8,17},{9,1... | collective-permute-start | bytes 442376
  423.4 43.6 %collective-permute-start.15 = (f32[96,384]{1,0:T(8,128)S(1)}, f32[96,384]{1,0:T(8,128)S(1)}, u32[]{:S(2)}, u32[]{:S(2)}) collective-permute-start(f32[96,384]{1,0:T(8,128)S(1)} %fusion), channel_id=1, source_target_pairs={{0,10},{1,11},{2,12},{3,13},{4,14},{5,15},{6,16},{7,17},{8,18},{9,... | collective-permute-start | bytes 442376
  434.1 42.3 %collective-permute-start.16 = (f32[96,384]{1,0:T(8,128)S(1)}, f32[96,384]{1,0:T(8,128)S(1)}, u32[]{:S(2)}, u32[]{:S(2)}) collective-permute-start(f32[96,384]{1,0:T(8,128)S(1)} %fusion), channel_id=1, source_target_pairs={{0,11},{1,12},{2,13},{3,14},{4,15},{5,16},{6,17},{7,18},{8,19},{9,... | collective-permute-start | bytes 442376
  435.4 50.2 %collective-permute-start.17 = (f32[96,384]{1,0:T(8,128)S(1)}, f32[96,384]{1,0:T(8,128)S(1)}, u32[]{:S(2)}, u32[]{:S(2)}) collective-permute-start(f32[96,384]{1,0:T(8,128)S(1)} %fusion), channel_id=1, source_target_pairs={{0,12},{1,13},{2,14},{3,15},{4,16},{5,17},{6,18},{7,19},{8,20},{9,... | collective-permute-start | bytes 442376
  436.7 51.5 %collective-permute-start.18 = (f32[96,384]{1,0:T(8,128)S(1)}, f32[96,384]{1,0:T(8,128)S(1)}, u32[]{:S(2)}, u32[]{:S(2)}) collective-permute-start(f32[96,384]{1,0:T(8,128)S(1)} %fusion), channel_id=1, source_target_pairs={{0,13},{1,14},{2,15},{3,16},{4,17},{5,18},{6,19},{7,20},{8,21},{9,... | collective-permute-start | bytes 442376
  438.1 70.6 %copy-start.3 = (f32[96,384]{1,0:T(8,128)S(1)}, f32[96,384]{1,0:T(8,128)}, u32[]{:S(2)}) copy-start(f32[96,384]{1,0:T(8,128)} %copy-done.2) | copy-start | bytes 442372
  438.1 70.6 %copy-start.5 = (f32[96,384]{1,0:T(8,128)S(1)}, f32[96,384]{1,0:T(8,128)}, u32[]{:S(2)}) copy-start(f32[96,384]{1,0:T(8,128)} %copy-done.4) | copy-start | bytes 442372
  458.9 48.4 %copy-start.6 = (f32[96,384]{1,0:T(8,128)}, f32[96,384]{1,0:T(8,128)S(1)}, u32[]{:S(2)}) copy-start(f32[96,384]{1,0:T(8,128)S(1)} %collective-permute-done.14) | copy-start | bytes 442372
  458.9 34.3 %collective-permute-start.19 = (f32[96,384]{1,0:T(8,128)S(1)}, f32[96,384]{1,0:T(8,128)S(1)}, u32[]{:S(2)}, u32[]{:S(2)}) collective-permute-start(f32[96,384]{1,0:T(8,128)S(1)} %fusion), channel_id=1, source_target_pairs={{0,14},{1,15},{2,16},{3,17},{4,18},{5,19},{6,20},{7,21},{8,22},{9,... | collective-permute-start | bytes 442376
  467.0 40.3 %copy-start.7 = (f32[96,384]{1,0:T(8,128)}, f32[96,384]{1,0:T(8,128)S(1)}, u32[]{:S(2)}) copy-start(f32[96,384]{1,0:T(8,128)S(1)} %collective-permute-done.15) | copy-start | bytes 442372
  467.0 27.5 %collective-permute-start.20 = (f32[96,384]{1,0:T(8,128)S(1)}, f32[96,384]{1,0:T(8,128)S(1)}, u32[]{:S(2)}, u32[]{:S(2)}) collective-permute-start(f32[96,384]{1,0:T(8,128)S(1)} %fusion), channel_id=1, source_target_pairs={{0,15},{1,16},{2,17},{3,18},{4,19},{5,20},{6,21},{7,22},{8,23},{9,... | collective-permute-start | bytes 442376
  476.4 30.9 %copy-start.8 = (f32[96,384]{1,0:T(8,128)}, f32[96,384]{1,0:T(8,128)S(1)}, u32[]{:S(2)}) copy-start(f32[96,384]{1,0:T(8,128)S(1)} %collective-permute-done.16) | copy-start | bytes 442372
  476.4 20.0 %collective-permute-start.21 = (f32[96,384]{1,0:T(8,128)S(1)}, f32[96,384]{1,0:T(8,128)S(1)}, u32[]{:S(2)}, u32[]{:S(2)}) collective-permute-start(f32[96,384]{1,0:T(8,128)S(1)} %fusion), channel_id=1, source_target_pairs={{0,16},{1,17},{2,18},{3,19},{4,20},{5,21},{6,22},{7,23},{8,24},{9,... | collective-permute-start | bytes 442376
  485.7 15.3 %collective-permute-start.22 = (f32[96,384]{1,0:T(8,128)S(1)}, f32[96,384]{1,0:T(8,128)S(1)}, u32[]{:S(2)}, u32[]{:S(2)}) collective-permute-start(f32[96,384]{1,0:T(8,128)S(1)} %fusion), channel_id=1, source_target_pairs={{0,17},{1,18},{2,19},{3,20},{4,21},{5,22},{6,23},{7,24},{8,25},{9,... | collective-permute-start | bytes 442376
  488.2 14.8 %collective-permute-start.23 = (f32[96,384]{1,0:T(8,128)S(1)}, f32[96,384]{1,0:T(8,128)S(1)}, u32[]{:S(2)}, u32[]{:S(2)}) collective-permute-start(f32[96,384]{1,0:T(8,128)S(1)} %fusion), channel_id=1, source_target_pairs={{0,18},{1,19},{2,20},{3,21},{4,22},{5,23},{6,24},{7,25},{8,26},{9,... | collective-permute-start | bytes 442376
  493.2 14.0 %collective-permute-start.24 = (f32[96,384]{1,0:T(8,128)S(1)}, f32[96,384]{1,0:T(8,128)S(1)}, u32[]{:S(2)}, u32[]{:S(2)}) collective-permute-start(f32[96,384]{1,0:T(8,128)S(1)} %fusion), channel_id=1, source_target_pairs={{0,19},{1,20},{2,21},{3,22},{4,23},{5,24},{6,25},{7,26},{8,27},{9,... | collective-permute-start | bytes 442376
  494.5 12.7 %collective-permute-start.6 = (f32[96,384]{1,0:T(8,128)S(1)}, f32[96,384]{1,0:T(8,128)S(1)}, u32[]{:S(2)}, u32[]{:S(2)}) collective-permute-start(f32[96,384]{1,0:T(8,128)S(1)} %fusion), channel_id=1, source_target_pairs={{0,1},{1,2},{2,3},{3,4},{4,5},{5,6},{6,7},{7,8},{8,9},{9,10},{10,1... | collective-permute-start | bytes 442376
  496.4 10.8 %collective-permute-start.7 = (f32[96,384]{1,0:T(8,128)S(1)}, f32[96,384]{1,0:T(8,128)S(1)}, u32[]{:S(2)}, u32[]{:S(2)}) collective-permute-start(f32[96,384]{1,0:T(8,128)S(1)} %fusion), channel_id=1, source_target_pairs={{0,2},{1,3},{2,4},{3,5},{4,6},{5,7},{6,8},{7,9},{8,10},{9,11},{10,... | collective-permute-start | bytes 442376
  501.0 6.3 %collective-permute-start.8 = (f32[96,384]{1,0:T(8,128)S(1)}, f32[96,384]{1,0:T(8,128)S(1)}, u32[]{:S(2)}, u32[]{:S(2)}) collective-permute-start(f32[96,384]{1,0:T(8,128)S(1)} %fusion), channel_id=1, source_target_pairs={{0,3},{1,4},{2,5},{3,6},{4,7},{5,8},{6,9},{7,10},{8,11},{9,12},{10... | collective-permute-start | bytes 442376
  503.1 5.6 %collective-permute-start.9 = (f32[96,384]{1,0:T(8,128)S(1)}, f32[96,384]{1,0:T(8,128)}, u32[]{:S(2)}, u32[]{:S(2)}) collective-permute-start(f32[96,384]{1,0:T(8,128)S(1)} %fusion), channel_id=1, source_target_pairs={{0,4},{1,5},{2,6},{3,7},{4,8},{5,9},{6,10},{7,11},{8,12},{9,13},{1... | collective-permute-start | bytes 442376
  (19 other events, 151.8 us)
where the time goes:
time: 538 us; the launch traced here: 528 us
  blocking collectives  394 us (73%)
  starting transfers between devices  82 us (15%)
  local copies, waits for them, and re-layouts  24.5 us (5%)
  matrix products  10.1 us (2%)
  waiting for transfers between devices  8.31 us (2%)
  other arithmetic  7.64 us (1%)
    unnamed x1, blocking collectives  361 us
    unnamed x20, starting transfers between devices  70.5 us
    unnamed x103, local copies, waits for them, and re-layouts  21.9 us
    psum x1, blocking collectives, per_device(): lax.psum((group_totals(grad_normed), group_totals(grad_normed * normed_bl...  17.3 us
    psum x1, blocking collectives, per_device(): lax.psum((group_totals(values), group_totals(values * values)), ('tm', 'r...  15.4 us
  transfers between devices with their start and end apart: 26, of which 4 were waited for; matrix products, arithmetic and copies ran while one was open for 72% of the time, Pallas kernels for 0%

commit v1 on v0

v1 whole, which is shorter than its diff:
```python
import jax
import jax.numpy as jnp
from jax import lax
from jax.experimental import pallas as pl
from jax.experimental.pallas import tpu as pltpu
from jax.sharding import PartitionSpec as P

MESH = pl.DeviceIdType.MESH
C = 384
SL = 48
PG = 12
POS = 1024
OWN = 256
EPS = 1e-05
CELLS = 12 * 2048
SCALE = 1.0 / 128
WIN1, HOP1, CUT1 = 168, 160, 88
WIN2, HOP2, CUT2 = 48, 40, 24
HALF = 648


def kernel(
    x_hbm, cot_hbm, w_hbm, gain_ref, shift_ref, ig_ref, wg_ref,
    x_own, x_send, x_all, cot, wv, gb, stat, normed_s, dsil_s, lcat, part,
    ig_send, ig_recv, d2m, d2p, bufm, bufp, res1, e2m, e2p, cufm, cufp, res2, fin,
    loc_sem, cs_send, cs_recv, xs_send, xs_recv, is_send, is_recv, r_send, r_recv, f_send, f_recv,
):
    clip, tm, rows = lax.axis_index("clip"), lax.axis_index("tm"), lax.axis_index("rows")
    x_hi, core = tm // 2, tm % 2
    j = tm * 2 + rows
    yy, zz = clip // 4, clip % 4

    def dev(tm_, rows_):
        return (clip, tm_, rows_)

    def ring(tm_, rows_, step):
        hi, co = tm_ // 2, tm_ % 2
        x = (hi * 2 + rows_ + step + 4) % 4
        return (x // 2) * 2 + co, x % 2

    rt, rr = ring(tm, rows, 1)
    lt, lr = ring(tm, rows, -1)
    ot, orow = ring(tm, rows, 2)
    sib_tm = x_hi * 2 + (1 - core)

    x_in = pltpu.make_async_copy(x_hbm, x_own, loc_sem.at[0])
    x_in.start()
    own_slot = pl.ds(pl.multiple_of(tm * OWN, OWN), OWN)
    c_in = pltpu.make_async_copy(cot_hbm, cot.at[rows, own_slot], loc_sem.at[1])
    c_in.start()
    w_in = pltpu.make_async_copy(
        w_hbm.at[:, pl.ds(pl.multiple_of(j * SL, SL), SL)], wv, loc_sem.at[2]
    )
    w_in.start()

    yp, ym = ((yy + 1) % 4) * 4 + zz, ((yy + 3) % 4) * 4 + zz
    zp, zm = yy * 4 + (zz + 1) % 4, yy * 4 + (zz + 3) % 4
    barrier = pltpu.get_barrier_semaphore()
    for k in range(1, 8):
        p = (j + k) % 8
        pl.semaphore_signal(barrier, inc=1, device_id=dev(p // 2, p % 2), device_id_type=MESH)
    for other in (yp, ym, zp, zm):
        pl.semaphore_signal(barrier, inc=1, device_id=(other, tm, rows), device_id_type=MESH)
    pl.semaphore_wait(barrier, 11)

    def frame(tm_, f):
        return pl.ds(pl.multiple_of(tm_ * OWN + f * 128, 128), 128)

    def cot_copy(slot, src, where, to):
        dst = cot.at[where[0], where[1]]
        return pltpu.make_async_remote_copy(
            src_ref=dst if src is None else src, dst_ref=dst,
            send_sem=cs_send.at[slot], recv_sem=cs_recv.at[slot],
            device_id=dev(*to), device_id_type=MESH,
        )

    right, left, sib = (rt, rr), (lt, lr), (sib_tm, rows)
    sends = []
    for slot, f, to in ((0, 0, right), (2, 1, left), (1, 1, right), (3, 0, left)):
        c = cot_copy(slot, cot_hbm.at[pl.ds(f * 128, 128)], (rows, frame(tm, f)), to)
        c.start()
        sends.append(c)
    c = cot_copy(4, cot_hbm, (rows, own_slot), sib)
    c.start()
    sends.append(c)

    def arrived(slot, where):
        cot_copy(slot, None, where, right).wait_recv()

    cot[0, POS:, :] = jnp.zeros((OWN, C), jnp.bfloat16)
    cot[1, POS:, :] = jnp.zeros((OWN, C), jnp.bfloat16)
    x_in.wait()
    x_send[...] = x_own[...].astype(jnp.float32).T.astype(jnp.bfloat16)
    own_lanes = pl.ds(pl.multiple_of(rows * POS + tm * OWN, OWN), OWN)
    x_self = pltpu.make_async_copy(
        x_send.at[pl.ds(pl.multiple_of(j * SL, SL), SL)], x_all.at[:, own_lanes], loc_sem.at[3]
    )
    x_self.start()
    xs = []
    for k in range(1, 8):
        p = (j + k) % 8
        c = pltpu.make_async_remote_copy(
            src_ref=x_send.at[pl.ds(pl.multiple_of(p * SL, SL), SL)], dst_ref=x_all.at[:, own_lanes],
            send_sem=xs_send.at[k - 1], recv_sem=xs_recv.at[k - 1],
            device_id=dev(p // 2, p % 2), device_id_type=MESH,
        )
        c.start()
        xs.append(c)

    gb[0] = jnp.broadcast_to(gain_ref[...], (128, C)).T
    gb[1] = jnp.broadcast_to(shift_ref[...], (128, C)).T
    mine = pl.ds(pl.multiple_of(j * SL, SL), SL)
    gain_l, shift_l = gb[0, mine, :], gb[1, mine, :]

    arrived(0, (lr, frame(lt, 0)))
    c = cot_copy(5, None, (lr, frame(lt, 0)), right)
    c.start()
    sends.append(c)
    arrived(2, (rr, frame(rt, 1)))
    c = cot_copy(6, None, (rr, frame(rt, 1)), left)
    c.start()
    sends.append(c)

    x_self.wait()
    for c in xs:
        c.wait_recv()

    row_g = lax.broadcasted_iota(jnp.int32, (SL, SL), 0)
    col_g = lax.broadcasted_iota(jnp.int32, (SL, SL), 1)

    def group_of(i):
        return sum((i >= PG * k).astype(jnp.int32) for k in (1, 2, 3))

    same = (group_of(row_g) == group_of(col_g)).astype(jnp.float32)

    def group_mean(values):
        total = jnp.sum(values, axis=1, keepdims=True)
        return jnp.dot(
            same, jnp.broadcast_to(total, (SL, 128)), precision=lax.Precision.HIGHEST,
            preferred_element_type=jnp.float32,
        ) * (1.0 / CELLS)

    s1 = jnp.zeros((SL, 128), jnp.float32)
    s2 = jnp.zeros((SL, 128), jnp.float32)
    for b in range(16):
        v = x_all[:, b * 128:(b + 1) * 128].astype(jnp.float32)
        s1 = s1 + v
        s2 = s2 + v * v
    mean = group_mean(s1)
    rstd = lax.rsqrt(group_mean(s2) - mean * mean + EPS)
    stat[...] = rstd

    lane = lax.broadcasted_iota(jnp.int32, (SL, 128), 1)
    for h in range(2):
        for dt in range(2):
            for dw in range(3):
                r0 = h * 432 + (dt * 3 + dw) * SL
                lcat[r0:r0 + SL, 0:(2 - dt) * 128] = jnp.zeros((SL, (2 - dt) * 128), jnp.bfloat16)
        for t in range(8):
            b = h * 8 + t
            sl = slice(b * 128, (b + 1) * 128)
            v = x_all[:, sl].astype(jnp.float32)
            normed = (v - mean) * rstd
            pre = normed * gain_l + shift_l
            s = 1.0 / (1.0 + jnp.exp(-pre))
            act = pre * s
            normed_s[:, sl] = normed
            dsil_s[:, sl] = s * (1.0 + pre * (1.0 - s)) * gain_l
            before = jnp.where(lane == 0, 0.0, pltpu.roll(act, 1, 1))
            after = jnp.where(lane == 127, 0.0, pltpu.roll(act, 127, 1))
            for dw, a in ((0, before), (1, act), (2, after)):
                a = a.astype(jnp.bfloat16)
                for dt in range(3):
                    t_out = t + 2 - dt
                    if t_out < 8:
                        r0 = h * 432 + (dt * 3 + dw) * SL
                        lcat[r0:r0 + SL, t_out * 128:(t_out + 1) * 128] = a

    arrived(1, (lr, frame(lt, 1)))
    arrived(3, (rr, frame(rt, 0)))
    for slot, who in ((7, (lt, lr)), (8, (rt, rr))):
        c = cot_copy(slot, None, (who[1], pl.ds(pl.multiple_of(who[0] * OWN, OWN), OWN)), sib)
        c.start()
        sends.append(c)
    arrived(5, (orow, frame(ot, 0)))
    arrived(6, (orow, frame(ot, 1)))
    c = cot_copy(9, None, (orow, pl.ds(pl.multiple_of(ot * OWN, OWN), OWN)), sib)
    c.start()
    sends.append(c)
    c_in.wait()

    def sib_of(who):
        t_ = who[0]
        return pl.ds(pl.multiple_of(((t_ // 2) * 2 + 1 - t_ % 2) * OWN, OWN), OWN)

    arrived(4, (rows, sib_of((tm, rows))))
    arrived(7, (lr, sib_of((lt, lr))))
    arrived(8, (rr, sib_of((rt, rr))))
    arrived(9, (orow, sib_of((ot, orow))))

    r_0 = jnp.dot(lcat[...], cot[0, 0:POS, :], preferred_element_type=jnp.float32)
    part[432:864] = r_0[0:432]
    part[864:1296] = r_0[432:864]
    r_1 = jnp.dot(lcat[...], cot[1, 0:POS, :], preferred_element_type=jnp.float32)
    part[0:432] = r_1[0:432]
    part[432:864] += r_1[432:864]

    def ring_copy(slot, src, dst, to):
        return pltpu.make_async_remote_copy(
            src_ref=src, dst_ref=dst, send_sem=r_send.at[slot], recv_sem=r_recv.at[slot],
            device_id=(to, tm, rows), device_id_type=MESH,
        )

    class Stage:
        def __init__(self, slot, src, base, win, hop, cut, pos, plus, minus, m2, p2, bm, bp, out):
            self.src, self.win, self.cut, self.out = src, win, cut, out
            self.bm, self.bp, self.m2, self.p2 = bm, bp, m2, p2

            def at(k, lo, hi):
                return pl.ds(pl.multiple_of(base + ((pos + k) % 4) * hop + lo, 8), hi - lo)

            self.at = at
            self.far_p = ring_copy(slot, src.at[at(2, 0, cut)], m2, plus)
            self.far_m = ring_copy(slot + 1, src.at[at(2, cut, win)], p2, minus)
            self.near_p = ring_copy(slot + 2, src.at[at(1, cut, win)], bm.at[pl.ds(cut, win - cut)], plus)
            self.near_m = ring_copy(slot + 3, src.at[at(3, 0, cut)], bp.at[pl.ds(0, cut)], minus)
            self.sum_p = ring_copy(slot + 4, m2, bm.at[pl.ds(0, cut)], plus)
            self.sum_m = ring_copy(slot + 5, p2, bp.at[pl.ds(cut, win - cut)], minus)
            self.all = (self.far_p, self.far_m, self.near_p, self.near_m, self.sum_p, self.sum_m)

        def start(self):
            for c in self.all[:4]:
                c.start()

        def middle(self):
            self.far_p.wait_recv()
            self.m2[...] += self.src[self.at(1, 0, self.cut), :]
            self.sum_p.start()
            self.far_m.wait_recv()
            self.p2[...] += self.src[self.at(3, self.cut, self.win), :]
            self.sum_m.start()

        def end(self):
            for c in self.all[2:]:
                c.wait_recv()
            self.out[...] = self.src[self.at(0, 0, self.win), :] + self.bm[...] + self.bp[...]

        def drain(self):
            for c in self.all:
                c.wait_send()

    first, second = [], []
    for a in range(2):
        along = ((yy, yp, ym), (zz, zp, zm))
        pos1, plus1, minus1 = along[a]
        pos2, plus2, minus2 = along[1 - a]
        first.append(Stage(
            a * 6, part, a * HALF, WIN1, HOP1, CUT1, pos1, plus1, minus1,
            d2m.at[a], d2p.at[a], bufm.at[a], bufp.at[a], res1.at[a],
        ))
        second.append(Stage(
            12 + a * 6, res1.at[a], 0, WIN2, HOP2, CUT2, pos2, plus2, minus2,
            e2m.at[a], e2p.at[a], cufm.at[a], cufp.at[a], res2.at[a],
        ))
    for st in first:
        st.start()

    w_in.wait()
    pick = (
        lax.broadcasted_iota(jnp.int32, (SL, C), 1)
        == lax.broadcasted_iota(jnp.int32, (SL, C), 0) + j * SL
    ).astype(jnp.bfloat16)
    nt = (((1,), (1,)), ((), ()))
    grads, cots = [], []
    for h in range(2):
        acc = jnp.zeros((144, POS), jnp.float32)
        for hs in range(2):
            dh = h - hs + 1
            for dt in range(3):
                tap = dt * 9 + dh * 3
                w_rows = wv[tap:tap + 3].reshape(144, C)
                c_rows = cot[hs, (2 - dt) * 128:(2 - dt) * 128 + POS, :]
                if hs == h and dt == 2:
                    both = lax.dot_general(
                        jnp.concatenate([w_rows, pick], 0), c_rows, nt, preferred_element_type=jnp.float32
                    )
                    cots.append(both[144:192])
                    acc = acc + both[0:144]
                else:
                    acc = acc + lax.dot_general(w_rows, c_rows, nt, preferred_element_type=jnp.float32)
        grads.append(acc)

    for st in first:
        st.middle()

    t1 = jnp.zeros((SL, 128), jnp.float32)
    t2 = jnp.zeros((SL, 128), jnp.float32)
    for h in range(2):
        for t in range(8):
            sl = slice(t * 128, (t + 1) * 128)
            gl = slice((h * 8 + t) * 128, (h * 8 + t + 1) * 128)
            g0, g1, g2 = (grads[h][k * SL:(k + 1) * SL, sl] for k in range(3))
            g = (
                g1
                + jnp.where(lane == 127, 0.0, pltpu.roll(g0, 127, 1))
                + jnp.where(lane == 0, 0.0, pltpu.roll(g2, 1, 1))
            )
            gn = g * dsil_s[:, gl]
            dsil_s[:, gl] = gn
            t1 = t1 + gn
            t2 = t2 + gn * normed_s[:, gl]
    m1, m2 = group_mean(t1), group_mean(t2)
    rstd_l = stat[...]
    for h in range(2):
        for t in range(8):
            sl = slice(t * 128, (t + 1) * 128)
            gl = slice((h * 8 + t) * 128, (h * 8 + t + 1) * 128)
            out = cots[h][:, sl] + rstd_l * (dsil_s[:, gl] - m1 - normed_s[:, gl] * m2)
            ig_send[:, gl] = out.astype(jnp.bfloat16)

    ig_self = pltpu.make_async_copy(ig_send.at[:, own_lanes], ig_recv.at[mine], loc_sem.at[3])
    ig_self.start()
    igs = []
    for k in range(1, 8):
        p = (j + k) % 8
        lanes = pl.ds(pl.multiple_of((p % 2) * POS + (p // 2) * OWN, OWN), OWN)
        c = pltpu.make_async_remote_copy(
            src_ref=ig_send.at[:, lanes], dst_ref=ig_recv.at[mine],
            send_sem=is_send.at[k - 1], recv_sem=is_recv.at[k - 1],
            device_id=dev(p // 2, p % 2), device_id_type=MESH,
        )
        c.start()
        igs.append(c)

    for st in first:
        st.end()
    for st in second:
        st.start()
    ig_self.wait()
    for c in igs:
        c.wait_recv()
    ig_ref[...] = ig_recv[...].astype(jnp.float32).T.astype(jnp.bfloat16)
    for st in second:
        st.middle()
    for st in second:
        st.end()

    last = jnp.logical_and(yy == 3, zz == 3)
    me = clip * 8 + j

    def scatter(act):
        for a in range(2):
            far, near = ((yy, zz), (zz, yy))[a]

            def body(i, _, a=a, far=far, near=near):
                loc = a * 81 + 20 * far + 5 * near + i
                dh, r = loc // 54, loc % 54
                tap = ((r // 6) // 3) * 9 + dh * 3 + (r // 6) % 3
                tile = tap * 48 + 6 * j + r % 6
                c_to, u = tile // 81, tile % 81
                valid = jnp.logical_or(i < 5, last)
                j1 = jnp.minimum(u // 10, 7)
                twice = jnp.logical_and(valid, jnp.logical_and(u % 10 == 0, jnp.logical_and(u > 0, u < 80)))
                src = res2.at[a, pl.ds(pl.multiple_of(i * 8, 8), 8)]
                act(valid, src, c_to, j1, u - 10 * j1, a * 12 + i)
                act(twice, src, c_to, jnp.maximum(u // 10 - 1, 0), 10, a * 12 + 6 + i)
                return 0

            lax.fori_loop(0, 6, body, 0)

    def fin_copy(src, c_to, j_to, slot, sem):
        return pltpu.make_async_remote_copy(
            src_ref=src, dst_ref=fin.at[pl.ds(pl.multiple_of(slot * 8, 8), 8)],
            send_sem=f_send.at[sem], recv_sem=f_recv.at[0],
            device_id=(c_to, j_to // 2, j_to % 2), device_id_type=MESH,
        )

    def begin(cond, src, c_to, j_to, slot, sem):
        here = c_to * 8 + j_to == me

        @pl.when(jnp.logical_and(cond, here))
        def _():
            pltpu.make_async_copy(
                src, fin.at[pl.ds(pl.multiple_of(slot * 8, 8), 8)], f_recv.at[0]
            ).start()

        @pl.when(jnp.logical_and(cond, jnp.logical_not(here)))
        def _():
            fin_copy(src, c_to, j_to, slot, sem).start()

    def finish(cond, src, c_to, j_to, slot, sem):
        @pl.when(jnp.logical_and(cond, c_to * 8 + j_to != me))
        def _():
            fin_copy(src, c_to, j_to, slot, sem).wait_send()

    scatter(begin)

    for c in sends + xs + igs:
        c.wait_send()
    for st in first + second:
        st.drain()

    pltpu.make_async_copy(fin, fin, f_recv.at[0]).wait()
    for k in range(8):
        @pl.when(j == k)
        def _(k=k):
            wg_ref[...] = fin[k:k + 81, :] * SCALE
    scatter(finish)


def per_device(inputs, cotangent, weight, gain, shift_term):
    f32, bf16 = jnp.float32, jnp.bfloat16
    hbm = pl.BlockSpec(memory_space=pltpu.HBM)
    vmem = pl.BlockSpec(memory_space=pltpu.VMEM)
    dma = pltpu.SemaphoreType.DMA
    ig, wg = pl.pallas_call(
        kernel,
        out_shape=(
            jax.ShapeDtypeStruct((OWN, C), bf16),
            jax.ShapeDtypeStruct((81, C), f32),
        ),
        in_specs=[hbm, hbm, hbm, vmem, vmem],
        out_specs=(vmem, vmem),
        scratch_shapes=[
            pltpu.VMEM((OWN, C), bf16),
            pltpu.VMEM((C, OWN), bf16),
            pltpu.VMEM((SL, 2 * POS), bf16),
            pltpu.VMEM((2, POS + OWN, C), bf16),
            pltpu.VMEM((27, SL, C), bf16),
            pltpu.VMEM((2, C, 128), f32),
            pltpu.VMEM((SL, 128), f32),
            pltpu.VMEM((SL, 2 * POS), f32),
            pltpu.VMEM((SL, 2 * POS), f32),
            pltpu.VMEM((864, POS), bf16),
            pltpu.VMEM((1296, C), f32),
            pltpu.VMEM((SL, 2 * POS), bf16),
            pltpu.VMEM((C, OWN), bf16),
            pltpu.VMEM((2, CUT1, C), f32),
            pltpu.VMEM((2, WIN1 - CUT1, C), f32),
            pltpu.VMEM((2, WIN1, C), f32),
            pltpu.VMEM((2, WIN1, C), f32),
            pltpu.VMEM((2, WIN1, C), f32),
            pltpu.VMEM((2, CUT2, C), f32),
            pltpu.VMEM((2, WIN2 - CUT2, C), f32),
            pltpu.VMEM((2, WIN2, C), f32),
            pltpu.VMEM((2, WIN2, C), f32),
            pltpu.VMEM((2, WIN2, C), f32),
            pltpu.VMEM((88, C), f32),
            dma((4,)), dma((10,)), dma((10,)), dma((7,)), dma((7,)), dma((7,)), dma((7,)),
            dma((24,)), dma((24,)), dma((24,)), dma((1,)),
        ],
        compiler_params=pltpu.CompilerParams(
            collective_id=0, has_side_effects=True, vmem_limit_bytes=56 * 1024 * 1024
        ),
        name="resblock_backward",
    )(
        inputs.reshape(OWN, C),
        cotangent.reshape(OWN, C),
        weight.reshape(27, C, C),
        gain.reshape(1, C),
        shift_term.reshape(1, C),
    )
    return ig.reshape(1, 2, 1, 128, C), wg


def solution(mesh):
    return jax.shard_map(
        per_device,
        mesh=mesh,
        in_specs=(
            P("clip", "tm", "rows", None, None),
            P("clip", "tm", "rows", None, None),
            P(),
            P(),
            P(),
        ),
        out_specs=(P("clip", "tm", "rows", None, None), P(("clip", "tm", "rows"), None)),
        check_vma=False,
    )
```

time: 538 us -> 54.7 us (0.10); the launches traced: 528 us -> 54.3 us
  blocking collectives: 394 us -> 0 us
  starting transfers between devices: 82 us -> 0 us
  Pallas kernels: 0 us -> 48 us
  local copies, waits for them, and re-layouts: 24.5 us -> 5.68 us
  matrix products: 10.1 us -> 0 us
  waiting for transfers between devices: 8.31 us -> 0 us
  other arithmetic: 7.64 us -> 0 us
    unnamed x1 -> x0, blocking collectives: 361 us -> none
    unnamed x20 -> x0, starting transfers between devices: 70.5 us -> none
    pallas_call x0 -> x1, Pallas kernels: none -> 48 us  [per_device(): pl.pallas_call(kernel, out_shape=(jax.ShapeDtypeStruct((OWN, C), bf16), j...]
    psum x2 -> x0, blocking collectives: 32.7 us -> none  [the longest x1 17.3 us: per_device(): lax.psum((group_totals(grad_normed), group_totals(grad_normed * normed_bl...]
    unnamed x103 -> x2, local copies, waits for them, and re-layouts: 21.9 us -> 3.19 us
    ppermute x6 -> x0, starting transfers between devices: 11.4 us -> none  [the longest x2 4.72 us: from_behind(): return lax.ppermute(block, axis, route)]
    dot_general x2 -> x0, matrix products: 10.1 us -> none  [the longest x1 7.1 us: per_device(): lax.dot_general(act_patch, cot_rows, (((0,), (0,)), ((), ())), preferred_...]
    ppermute x6 -> x0, waiting for transfers between devices: 7.27 us -> none  [the longest x2 3.94 us: with_halo(): after = lax.ppermute(first, axis, down)]
  transfers between devices with their start and end apart: 26 -> 0, of which waited for: 4 -> 0; matrix products, arithmetic and copies ran while one was open for 72% -> 0% of each run, Pallas kernels for 0% -> 0%
where the time goes in v1:
time: 54.7 us; the launch traced here: 54.3 us
  Pallas kernels  48 us (88%)
  local copies, waits for them, and re-layouts  5.68 us (10%)
  between operations  0.64 us (1%)
    pallas_call x1, Pallas kernels, per_device(): pl.pallas_call(kernel, out_shape=(jax.ShapeDtypeStruct((OWN, C), bf16), j...  48 us
    unnamed x2, local copies, waits for them, and re-layouts  3.19 us
    reshape x1, local copies, waits for them, and re-layouts, per_device(): gain.reshape(1, C)  1.25 us
    reshape x1, local copies, waits for them, and re-layouts, per_device(): shift_term.reshape(1, C)  1.24 us

profile of v1, /device:TPU:1, one launch (start us, length us, event | category | flops | bytes accessed | tf_op | source)
XLA Modules:
  0.0 54.3 jit_solution(11138299562431265313)
XLA Ops:
  0.6 1.2 %reshape.25.gain_ref = f32[1,384]{1,0:T(1,128)} reshape(f32[384]{0:T(512)} %param.8) | data formatting | bytes 3072 | tf_op jit(solution)/shard_map/reshape | solution.py:460
  1.9 1.2 %reshape.26.shift_ref = f32[1,384]{1,0:T(1,128)} reshape(f32[384]{0:T(512)} %param.9) | data formatting | bytes 3072 | tf_op jit(solution)/shard_map/reshape | solution.py:461
  3.1 48.0 %resblock_backward.1 = (bf16[256,384]{1,0:T(8,128)(2,1)}, f32[81,384]{1,0:T(8,128)}) custom-call(bf16[256,384]{1,0:T(8,128)(2,1)} %bitcast.8, bf16[256,384]{1,0:T(8,128)(2,1)} %bitcast.9, bf16[27,384,384]{2,1,0:T(8,128)(2,1)} %bitcast.6, f32[1,384]{1,0:T(1,128)} %reshape.25.gain_ref, f32[1,384]{1,0:T(1,128)} %reshape.26.shift_ref), custom_call_target="tpu_custom_call" | custom-call | tf_op jit(solution)/shard_map/resblock_backward/pallas_call | solution.py:416
  51.1 1.6 %copy.10 = bf16[1,2,1,128,384]{4,3,2,1,0:T(8,128)(2,1)} copy(bf16[1,2,1,128,384]{4,3,2,1,0:T(8,128)(2,1)} %bitcast.7) | data formatting | bytes 393216
  52.7 1.6 %copy.11 = f32[81,384]{1,0:T(8,128)} copy(f32[81,384]{1,0:T(8,128)} %get-tuple-element.11) | data formatting | bytes 248832

commit v2 on v1

--- a/solution.py
+++ b/solution.py
@@ -20,9 +20,9 @@
 
 
 def kernel(
-    x_hbm, cot_hbm, w_hbm, gain_ref, shift_ref, ig_ref, wg_ref,
+    x_hbm, cot_hbm, w_hbm, gain_ref, shift_ref, ig_ref, fin,
     x_own, x_send, x_all, cot, wv, gb, stat, normed_s, dsil_s, lcat, part,
-    ig_send, ig_recv, d2m, d2p, bufm, bufp, res1, e2m, e2p, cufm, cufp, res2, fin,
+    ig_send, ig_recv, d2m, d2p, bufm, bufp, res1, e2m, e2p, cufm, cufp, res2,
     loc_sem, cs_send, cs_recv, xs_send, xs_recv, is_send, is_recv, r_send, r_recv, f_send, f_recv,
 ):
     clip, tm, rows = lax.axis_index("clip"), lax.axis_index("tm"), lax.axis_index("rows")
@@ -107,8 +107,8 @@
         c.start()
         xs.append(c)
 
-    gb[0] = jnp.broadcast_to(gain_ref[...], (128, C)).T
-    gb[1] = jnp.broadcast_to(shift_ref[...], (128, C)).T
+    gb[0] = jnp.broadcast_to(gain_ref[...].reshape(1, C), (128, C)).T
+    gb[1] = jnp.broadcast_to(shift_ref[...].reshape(1, C), (128, C)).T
     mine = pl.ds(pl.multiple_of(j * SL, SL), SL)
     gain_l, shift_l = gb[0, mine, :], gb[1, mine, :]
 
@@ -401,11 +401,18 @@
         st.drain()
 
     pltpu.make_async_copy(fin, fin, f_recv.at[0]).wait()
+    scatter(finish)
+
+
+def write_out(ig_in, fin, ig_out, wg_out, sem):
+    copy = pltpu.make_async_copy(ig_in, ig_out, sem)
+    copy.start()
+    j = lax.axis_index("tm") * 2 + lax.axis_index("rows")
     for k in range(8):
         @pl.when(j == k)
         def _(k=k):
-            wg_ref[...] = fin[k:k + 81, :] * SCALE
-    scatter(finish)
+            wg_out[...] = fin[k:k + 81, :] * SCALE
+    copy.wait()
 
 
 def per_device(inputs, cotangent, weight, gain, shift_term):
@@ -413,12 +420,9 @@
     hbm = pl.BlockSpec(memory_space=pltpu.HBM)
     vmem = pl.BlockSpec(memory_space=pltpu.VMEM)
     dma = pltpu.SemaphoreType.DMA
-    ig, wg = pl.pallas_call(
+    ig, fin = pl.pallas_call(
         kernel,
-        out_shape=(
-            jax.ShapeDtypeStruct((OWN, C), bf16),
-            jax.ShapeDtypeStruct((81, C), f32),
-        ),
+        out_shape=(pltpu.VMEM((OWN, C), bf16), pltpu.VMEM((88, C), f32)),
         in_specs=[hbm, hbm, hbm, vmem, vmem],
         out_specs=(vmem, vmem),
         scratch_shapes=[
@@ -445,7 +449,6 @@
             pltpu.VMEM((2, WIN2, C), f32),
             pltpu.VMEM((2, WIN2, C), f32),
             pltpu.VMEM((2, WIN2, C), f32),
-            pltpu.VMEM((88, C), f32),
             dma((4,)), dma((10,)), dma((10,)), dma((7,)), dma((7,)), dma((7,)), dma((7,)),
             dma((24,)), dma((24,)), dma((24,)), dma((1,)),
         ],
@@ -457,9 +460,21 @@
         inputs.reshape(OWN, C),
         cotangent.reshape(OWN, C),
         weight.reshape(27, C, C),
-        gain.reshape(1, C),
-        shift_term.reshape(1, C),
+        gain,
+        shift_term,
     )
+    ig, fin = (pltpu.with_memory_space_constraint(v, pltpu.VMEM) for v in (ig, fin))
+    ig, wg = pl.pallas_call(
+        write_out,
+        out_shape=(
+            jax.ShapeDtypeStruct((OWN, C), bf16),
+            jax.ShapeDtypeStruct((81, C), f32),
+        ),
+        in_specs=[vmem, vmem],
+        out_specs=(hbm, vmem),
+        scratch_shapes=[dma],
+        name="write_out",
+    )(ig, fin)
     return ig.reshape(1, 2, 1, 128, C), wg
 
 

time: 54.7 us -> 48.9 us (0.89)
  local copies, waits for them, and re-layouts: 5.68 us -> 0 us
    unnamed x2 -> x0, local copies, waits for them, and re-layouts: 3.19 us -> none
    reshape x2 -> x0, local copies, waits for them, and re-layouts: 2.49 us -> none  [the longest x1 1.25 us: per_device(): gain.reshape(1, C)]
    pallas_call x1 -> x2, Pallas kernels: 48 us -> 48 us  [the longest x1 46.6 us: per_device(): pl.pallas_call(kernel, out_shape=(pltpu.VMEM((OWN, C), bf16), pltpu.VMEM(...]
where the time goes in v2:
time: 48.9 us; the launch traced here: 48.6 us
  Pallas kernels  48 us (98%)
  between operations  0.64 us (1%)
    pallas_call x1, Pallas kernels, per_device(): pl.pallas_call(kernel, out_shape=(pltpu.VMEM((OWN, C), bf16), pltpu.VMEM(...  46.6 us
    pallas_call x1, Pallas kernels, per_device(): pl.pallas_call(write_out, out_shape=(jax.ShapeDtypeStruct((OWN, C), bf16)...  1.34 us

profile of v2, /device:TPU:1, one launch (start us, length us, event | category | flops | bytes accessed | tf_op | source)
XLA Modules:
  0.0 48.6 jit_solution(9577451570173726516)
XLA Ops:
  0.6 46.6 %resblock_backward.1 = (bf16[256,384]{1,0:T(8,128)(2,1)S(1)}, f32[88,384]{1,0:T(8,128)S(1)}) custom-call(bf16[256,384]{1,0:T(8,128)(2,1)} %bitcast.7, bf16[256,384]{1,0:T(8,128)(2,1)} %bitcast.8, bf16[27,384,384]{2,1,0:T(8,128)(2,1)} %bitcast.6, f32[384]{0:T(512)} %gain_ref.1, f32[384]{0:T(512)} %shift_ref.1), custom_call_target="tpu_custom_call" | custom-call | tf_op jit(solution)/shard_map/resblock_backward/pallas_call | solution.py:423
  47.3 1.3 %write_out.1 = (bf16[256,384]{1,0:T(8,128)(2,1)}, f32[81,384]{1,0:T(8,128)}) custom-call(bf16[256,384]{1,0:T(8,128)(2,1)S(1)} %get-tuple-element.6.ig_in, f32[88,384]{1,0:T(8,128)S(1)} %get-tuple-element.7.fin), custom_call_target="tpu_custom_call" | custom-call | tf_op jit(solution)/shard_map/write_out/pallas_call | solution.py:467

commit v3 on v2

v3 whole, which is shorter than its diff:
```python
import jax
import jax.numpy as jnp
from jax import lax
from jax.experimental import pallas as pl
from jax.experimental.pallas import tpu as pltpu
from jax.sharding import PartitionSpec as P

MESH = pl.DeviceIdType.MESH
C = 384
SL = 48
PG = 12
POS = 1024
OWN = 256
EPS = 1e-05
CELLS = 12 * 2048
SCALE = 1.0 / 128
ODD = (1, 7, 13, 21, 9, 15, 23, 3, 11, 17, 5, 19, 25)
ORDER = tuple(range(0, 27, 2)) + ODD
WIN1, CUT1 = 168, 88
BASES, HOPS = (0, 672), (168, 152)
WIN2, HOP2 = 48, 40
GCH = ((0, 384),)
NG = len(GCH)
CH = ((0, 384),)
NCH = len(CH)


MSG = 96
SPAN = 125.0


def encode(values):
    n, w = values.shape
    tiles = values.reshape(n // 8, 8, w)
    top = jnp.max(jnp.abs(tiles), axis=0) * 1.01 + 1e-30
    top = top.astype(jnp.bfloat16).astype(jnp.float32)
    code = jnp.exp2(tiles * (SPAN / top)[None]).reshape(n, w)
    return jnp.concatenate([code] + [top] * ((MSG - n) // 8), 0).astype(jnp.bfloat16)


def decode(message, n):
    wide = message.astype(jnp.float32)
    top = wide[n:n + 8] * (1.0 / SPAN)
    w = wide.shape[1]
    return (jnp.log2(wide[0:n]).reshape(n // 8, 8, w) * top[None]).reshape(n, w)


def kernel(
    x_hbm, cot_hbm, w_hbm, gain_ref, shift_ref, ig_ref, fin,
    x_own, x_send, x_all, cot, wv, gb, stat, normed_s, dsil_s, lcat, part,
    ig_send, ig_recv, out_b, in_b, res1, ebuf, res2,
    loc_sem, cs_send, cs_recv, xs_send, xs_recv, is_send, is_recv, r_send, r_recv, f_send, f_recv,
):
    clip, tm, rows = lax.axis_index("clip"), lax.axis_index("tm"), lax.axis_index("rows")
    x_hi, core = tm // 2, tm % 2
    j = tm * 2 + rows
    yy, zz = clip // 4, clip % 4

    def dev(tm_, rows_):
        return (clip, tm_, rows_)

    def ring(tm_, rows_, step):
        hi, co = tm_ // 2, tm_ % 2
        x = (hi * 2 + rows_ + step + 4) % 4
        return (x // 2) * 2 + co, x % 2

    rt, rr = ring(tm, rows, 1)
    lt, lr = ring(tm, rows, -1)
    ot, orow = ring(tm, rows, 2)
    sib_tm = x_hi * 2 + (1 - core)

    x_in = pltpu.make_async_copy(x_hbm, x_own, loc_sem.at[0])
    x_in.start()
    own_slot = pl.ds(pl.multiple_of(tm * OWN, OWN), OWN)
    c_in = []
    for c in range(NG):
        copy = pltpu.make_async_copy(
            cot_hbm.at[:, pl.ds(*GCH[c])], cot.at[rows, own_slot, pl.ds(*GCH[c])], loc_sem.at[4 + c]
        )
        copy.start()
        c_in.append(copy)
    w_in = pltpu.make_async_copy(
        w_hbm.at[:, pl.ds(pl.multiple_of(j * SL, SL), SL)], wv, loc_sem.at[2]
    )
    w_in.start()

    yp, ym = ((yy + 1) % 4) * 4 + zz, ((yy + 3) % 4) * 4 + zz
    yo, zo = ((yy + 2) % 4) * 4 + zz, yy * 4 + (zz + 2) % 4
    zp, zm = yy * 4 + (zz + 1) % 4, yy * 4 + (zz + 3) % 4
    barrier = pltpu.get_barrier_semaphore()
    for k in range(1, 8):
        p = (j + k) % 8
        pl.semaphore_signal(barrier, inc=1, device_id=dev(p // 2, p % 2), device_id_type=MESH)
    for other in (yp, ym, zp, zm):
        pl.semaphore_signal(barrier, inc=1, device_id=(other, tm, rows), device_id_type=MESH)

    x_in.wait()
    x_send[...] = x_own[...].astype(jnp.float32).T.astype(jnp.bfloat16)
    gb[0] = jnp.broadcast_to(gain_ref[...].reshape(1, C), (128, C)).T
    gb[1] = jnp.broadcast_to(shift_ref[...].reshape(1, C), (128, C)).T
    for h in range(2):
        cot[h, POS:, :] = jnp.zeros((OWN, C), jnp.bfloat16)
    pl.semaphore_wait(barrier, 11)

    def frame(tm_, f):
        return pl.ds(pl.multiple_of(tm_ * OWN + f * 128, 128), 128)

    def cot_copy(ch, slot, where, to):
        ref = cot.at[where[0], where[1], pl.ds(*GCH[ch])]
        return pltpu.make_async_remote_copy(
            src_ref=ref, dst_ref=ref,
            send_sem=cs_send.at[ch, slot], recv_sem=cs_recv.at[ch, slot],
            device_id=dev(*to), device_id_type=MESH,
        )

    right, left, sib = (rt, rr), (lt, lr), (sib_tm, rows)
    sends = []

    def send(ch, slot, where, to):
        copy = cot_copy(ch, slot, where, to)
        copy.start()
        sends.append(copy)

    def arrived(ch, slot, where):
        cot_copy(ch, slot, where, right).wait_recv()

    def whole(who):
        return who[1], pl.ds(pl.multiple_of(who[0] * OWN, OWN), OWN)

    def sib_of(who):
        return whole((who[0] + 1 - 2 * (who[0] % 2), who[1]))

    def own(ch):
        c_in[ch].wait()
        send(ch, 0, (rows, frame(tm, 0)), right)
        send(ch, 2, (rows, frame(tm, 1)), left)
        send(ch, 1, (rows, frame(tm, 1)), right)
        send(ch, 3, (rows, frame(tm, 0)), left)
        send(ch, 4, (rows, own_slot), sib)

    def fwd1(ch):
        arrived(ch, 0, (lr, frame(lt, 0)))
        send(ch, 5, (lr, frame(lt, 0)), right)
        arrived(ch, 2, (rr, frame(rt, 1)))
        send(ch, 6, (rr, frame(rt, 1)), left)

    def fwd2(ch):
        arrived(ch, 1, (lr, frame(lt, 1)))
        send(ch, 7, whole((lt, lr)), sib)
        arrived(ch, 3, (rr, frame(rt, 0)))
        send(ch, 8, whole((rt, rr)), sib)

    def fwd3(ch):
        arrived(ch, 5, (orow, frame(ot, 0)))
        arrived(ch, 6, (orow, frame(ot, 1)))
        send(ch, 9, whole((ot, orow)), sib)

    def gathered(ch):
        arrived(ch, 4, sib_of((tm, rows)))
        arrived(ch, 7, sib_of((lt, lr)))
        arrived(ch, 8, sib_of((rt, rr)))
        arrived(ch, 9, sib_of((ot, orow)))

    own(0)

    own_lanes = pl.ds(pl.multiple_of(rows * POS + tm * OWN, OWN), OWN)
    x_self = pltpu.make_async_copy(
        x_send.at[pl.ds(pl.multiple_of(j * SL, SL), SL)], x_all.at[:, own_lanes], loc_sem.at[3]
    )
    x_self.start()
    xs = []
    for k in range(1, 8):
        p = (j + k) % 8
        c = pltpu.make_async_remote_copy(
            src_ref=x_send.at[pl.ds(pl.multiple_of(p * SL, SL), SL)], dst_ref=x_all.at[:, own_lanes],
            send_sem=xs_send.at[k - 1], recv_sem=xs_recv.at[k - 1],
            device_id=dev(p // 2, p % 2), device_id_type=MESH,
        )
        c.start()
        xs.append(c)

    mine = pl.ds(pl.multiple_of(j * SL, SL), SL)
    gain_l, shift_l = gb[0, mine, :], gb[1, mine, :]

    fwd1(0)

    me = clip * 8 + j
    jobs = []
    for a in range(2):
        far, near = ((yy, zz), (zz, yy))[a]
        again = []
        for i in range(6):
            loc = (21, 19)[a] * far + 5 * near + i
            n = loc // 6
            tap = 2 * n if a == 0 else sum(jnp.where(n == k, t, 0) for k, t in enumerate(ODD))
            r = loc % 6
            tile = tap * 48 + 6 * j + r
            c_to, u = tile // 81, tile % 81
            j_to = jnp.minimum(u // 10, 7)
            if i < 4:
                ok = jnp.bool_(True)
            elif a == 0:
                ok = jnp.logical_or(i < 5, near == 3)
            elif i == 4:
                ok = jnp.logical_or(near < 3, far == 3)
            else:
                ok = jnp.logical_and(near == 3, far == 3)
            jobs.append((ok, c_to * 8 + j_to, u - 10 * j_to))
            edge = jnp.logical_and(u - 10 * j_to == 0, j_to > 0)
            again.append((jnp.logical_and(ok, edge), c_to * 8 + jnp.maximum(j_to - 1, 0), 10))
        jobs += again

    x_self.wait()
    for c in xs:
        c.wait_recv()

    row_g = lax.broadcasted_iota(jnp.int32, (SL, SL), 0)
    col_g = lax.broadcasted_iota(jnp.int32, (SL, SL), 1)

    def group_of(i):
        return sum((i >= PG * k).astype(jnp.int32) for k in (1, 2, 3))

    same = (group_of(row_g) == group_of(col_g)).astype(jnp.float32)

    def group_mean(values):
        total = jnp.sum(values, axis=1, keepdims=True)
        return jnp.dot(
            same, jnp.broadcast_to(total, (SL, 128)), precision=lax.Precision.HIGHEST,
            preferred_element_type=jnp.float32,
        ) * (1.0 / CELLS)

    s1 = jnp.zeros((SL, 128), jnp.float32)
    s2 = jnp.zeros((SL, 128), jnp.float32)
    for b in range(16):
        v = x_all[:, b * 128:(b + 1) * 128].astype(jnp.float32)
        s1 = s1 + v
        s2 = s2 + v * v
    mean = group_mean(s1)
    rstd = lax.rsqrt(group_mean(s2) - mean * mean + EPS)
    stat[...] = rstd

    lane = lax.broadcasted_iota(jnp.int32, (SL, 128), 1)
    for h in range(2):
        for dt in range(2):
            for dw in range(3):
                r0 = h * 432 + (dt * 3 + dw) * SL
                lcat[r0:r0 + SL, 0:(2 - dt) * 128] = jnp.zeros((SL, (2 - dt) * 128), jnp.bfloat16)
        for t in range(8):
            b = h * 8 + t
            sl = slice(b * 128, (b + 1) * 128)
            v = x_all[:, sl].astype(jnp.float32)
            normed = (v - mean) * rstd
            pre = normed * gain_l + shift_l
            s = 1.0 / (1.0 + jnp.exp(-pre))
            act = pre * s
            normed_s[:, sl] = normed
            dsil_s[:, sl] = s * (1.0 + pre * (1.0 - s)) * gain_l
            before = jnp.where(lane == 0, 0.0, pltpu.roll(act, 1, 1))
            after = jnp.where(lane == 127, 0.0, pltpu.roll(act, 127, 1))
            for dw, a in ((0, before), (1, act), (2, after)):
                a = a.astype(jnp.bfloat16)
                for dt in range(3):
                    t_out = t + 2 - dt
                    if t_out < 8:
                        r0 = h * 432 + (dt * 3 + dw) * SL
                        lcat[r0:r0 + SL, t_out * 128:(t_out + 1) * 128] = a

    def weight_grad(ch):
        lo, hi = CH[ch][0], sum(CH[ch])
        r_0 = jnp.dot(lcat[...], cot[0, 0:POS, lo:hi], preferred_element_type=jnp.float32)
        r_1 = jnp.dot(lcat[...], cot[1, 0:POS, lo:hi], preferred_element_type=jnp.float32)
        for dt in range(3):
            for dw in range(3):
                q = (dt * 3 + dw) * SL
                near = [r[k:k + SL] for r in (r_0, r_1) for k in (q, q + 432)]
                for dh, v in ((0, near[2]), (1, near[0] + near[3]), (2, near[1])):
                    r0 = ORDER.index(dt * 9 + dh * 3 + dw) * SL
                    part[r0:r0 + SL, lo:hi] = v

    def ring_copy(ch, slot, src, dst, to):
        return pltpu.make_async_remote_copy(
            src_ref=src, dst_ref=dst, send_sem=r_send.at[ch, slot], recv_sem=r_recv.at[ch, slot],
            device_id=(to, tm, rows), device_id_type=MESH,
        )

    class Ring:
        def __init__(self, ch, slot, src, base, hop, pos, plus, minus, out_b, in_b, out):
            self.src, self.out, self.out_b, self.in_b = src, out, out_b, in_b

            def at(k, lo, hi):
                return pl.ds(pl.multiple_of(base + ((pos + k) % 4) * hop + lo, 8), hi - lo)

            self.at = at
            self.all = [
                ring_copy(ch, slot + k, out_b.at[k], in_b.at[k], minus if k % 2 else plus) for k in range(6)
            ]

        def put(self, k, values):
            self.out_b[k] = encode(values)
            self.all[k].start()

        def got(self, k, n):
            self.all[k].wait_recv()
            return decode(self.in_b[k], n)

        def start(self):
            self.put(0, self.src[self.at(2, 0, CUT1), :])
            self.put(1, self.src[self.at(2, CUT1, WIN1), :])

        def near(self):
            self.put(2, self.src[self.at(1, CUT1, WIN1), :])
            self.put(3, self.src[self.at(3, 0, CUT1), :])

        def middle(self):
            self.put(4, self.got(0, CUT1) + self.src[self.at(1, 0, CUT1), :])
            self.put(5, self.got(1, WIN1 - CUT1) + self.src[self.at(3, CUT1, WIN1), :])

        def end(self):
            self.out[0:CUT1] = self.src[self.at(0, 0, CUT1), :] + self.got(3, CUT1) + self.got(4, CUT1)
            self.out[CUT1:WIN1] = (
                self.src[self.at(0, CUT1, WIN1), :] + self.got(2, WIN1 - CUT1) + self.got(5, WIN1 - CUT1)
            )

    class Direct:
        def __init__(self, ch, slot, src, pos, to, bufs, out):
            self.src, self.bufs, self.out = src, bufs, out
            self.at = [pl.ds(pl.multiple_of(((pos + k) % 4) * HOP2, 8), WIN2) for k in range(4)]
            self.all = [
                ring_copy(ch, slot + k - 1, src.at[self.at[k]], bufs.at[k - 1], to[k - 1]) for k in (2, 1, 3)
            ]

        def start(self):
            for c in self.all:
                c.start()

        def end(self):
            for c in self.all:
                c.wait_recv()
            self.out[...] = self.src[self.at[0], :] + self.bufs[0] + self.bufs[1] + self.bufs[2]

    first, second = [], []
    for c in range(NCH):
        for a in range(2):
            lanes = pl.ds(*CH[c])
            along = ((yy, yp, ym, yo), (zz, zp, zm, zo))
            pos1, plus1, minus1, _ = along[a]
            pos2, plus2, minus2, far2 = along[1 - a]
            first.append(Ring(
                c, a * 6, part.at[:, lanes], BASES[a], HOPS[a], pos1, plus1, minus1,
                out_b.at[a, :, :, lanes], in_b.at[a, :, :, lanes], res1.at[a, :, lanes],
            ))
            second.append(Direct(
                c, 12 + a * 3, res1.at[a, :, lanes], pos2, (plus2, far2, minus2),
                ebuf.at[a, :, :, lanes], res2.at[a, :, lanes],
            ))

    def start1(ch):
        for st in first[2 * ch:2 * ch + 2]:
            st.start()

    def near1(ch):
        for st in first[2 * ch:2 * ch + 2]:
            st.near()

    def mid1(ch):
        for st in first[2 * ch:2 * ch + 2]:
            st.middle()

    def turn(ch):
        for st, nxt in zip(first[2 * ch:2 * ch + 2], second[2 * ch:2 * ch + 2]):
            st.end()
            nxt.start()

    def end2(ch):
        for st in second[2 * ch:2 * ch + 2]:
            st.end()
        scatter(ch, begin)

    nt = (((1,), (1,)), ((), ()))
    grads, cots = [], []

    def grad_active(h):
        acc = jnp.zeros((144, POS), jnp.float32)
        for hs in range(2):
            dh = h - hs + 1
            for dt in range(3):
                tap = dt * 9 + dh * 3
                w_rows = wv[tap:tap + 3].reshape(144, C)
                c_rows = cot[hs, (2 - dt) * 128:(2 - dt) * 128 + POS, :]
                if hs == h and dt == 2:
                    both = lax.dot_general(
                        jnp.concatenate([w_rows, pick], 0), c_rows, nt, preferred_element_type=jnp.float32
                    )
                    cots.append(both[144:192])
                    acc = acc + both[0:144]
                else:
                    acc = acc + lax.dot_general(w_rows, c_rows, nt, preferred_element_type=jnp.float32)
        grads.append(acc)

    def input_grad():
        t1 = jnp.zeros((SL, 128), jnp.float32)
        t2 = jnp.zeros((SL, 128), jnp.float32)
        for h in range(2):
            for t in range(8):
                sl = slice(t * 128, (t + 1) * 128)
                gl = slice((h * 8 + t) * 128, (h * 8 + t + 1) * 128)
                g0, g1, g2 = (grads[h][k * SL:(k + 1) * SL, sl] for k in range(3))
                g = (
                    g1
                    + jnp.where(lane == 127, 0.0, pltpu.roll(g0, 127, 1))
                    + jnp.where(lane == 0, 0.0, pltpu.roll(g2, 1, 1))
                )
                gn = g * dsil_s[:, gl]
                dsil_s[:, gl] = gn
                t1 = t1 + gn
                t2 = t2 + gn * normed_s[:, gl]
        m1, m2 = group_mean(t1), group_mean(t2)
        rstd_l = stat[...]
        for h in range(2):
            for t in range(8):
                sl = slice(t * 128, (t + 1) * 128)
                gl = slice((h * 8 + t) * 128, (h * 8 + t + 1) * 128)
                out = cots[h][:, sl] + rstd_l * (dsil_s[:, gl] - m1 - normed_s[:, gl] * m2)
                ig_send[:, gl] = out.astype(jnp.bfloat16)

    ig_self = pltpu.make_async_copy(ig_send.at[:, own_lanes], ig_recv.at[mine], loc_sem.at[3])
    igs = []
    for k in range(1, 8):
        p = (j + k) % 8
        lanes = pl.ds(pl.multiple_of((p % 2) * POS + (p // 2) * OWN, OWN), OWN)
        igs.append(pltpu.make_async_remote_copy(
            src_ref=ig_send.at[:, lanes], dst_ref=ig_recv.at[mine],
            send_sem=is_send.at[k - 1], recv_sem=is_recv.at[k - 1],
            device_id=dev(p // 2, p % 2), device_id_type=MESH,
        ))

    def ig_out():
        ig_self.wait()
        for c in igs:
            c.wait_recv()
        ig_ref[...] = ig_recv[...].astype(jnp.float32).T.astype(jnp.bfloat16)

    def scatter(ch, act):
        for n, (ok, d_to, slot) in enumerate(jobs):
            src = res2.at[n // 12, pl.ds(n % 6 * 8, 8), pl.ds(*CH[ch])]
            act(ch, n, ok, src, d_to, slot)

    def fin_at(ch, slot):
        return fin.at[pl.ds(pl.multiple_of(slot * 8, 8), 8), pl.ds(*CH[ch])]

    def fin_copy(ch, n, src, d_to, slot):
        return pltpu.make_async_remote_copy(
            src_ref=src, dst_ref=fin_at(ch, slot), send_sem=f_send.at[ch, n], recv_sem=f_recv.at[ch],
            device_id=(d_to // 8, d_to % 8 // 2, d_to % 2), device_id_type=MESH,
        )

    def begin(ch, n, ok, src, d_to, slot):
        @pl.when(jnp.logical_and(ok, d_to == me))
        def _():
            pltpu.make_async_copy(src, fin_at(ch, slot), f_recv.at[ch]).start()

        @pl.when(jnp.logical_and(ok, d_to != me))
        def _():
            fin_copy(ch, n, src, d_to, slot).start()

    def finish(ch, n, ok, src, d_to, slot):
        @pl.when(jnp.logical_and(ok, d_to != me))
        def _():
            fin_copy(ch, n, src, d_to, slot).wait_send()

    fwd2(0)
    fwd3(0)
    gathered(0)
    weight_grad(0)
    start1(0)
    near1(0)
    w_in.wait()
    pick = (
        lax.broadcasted_iota(jnp.int32, (SL, C), 1)
        == lax.broadcasted_iota(jnp.int32, (SL, C), 0) + j * SL
    ).astype(jnp.bfloat16)
    grad_active(0)
    grad_active(1)
    mid1(0)
    input_grad()
    for c in [ig_self] + igs:
        c.start()
    turn(0)
    ig_out()
    end2(0)

    for c in sends + xs + igs:
        c.wait_send()
    for st in first + second:
        for c in st.all:
            c.wait_send()
    for c in range(NCH):
        lanes = fin.at[:, pl.ds(*CH[c])]
        pltpu.make_async_copy(lanes, lanes, f_recv.at[c]).wait()
    for c in range(NCH):
        scatter(c, finish)


def write_out(ig_in, fin, ig_out, wg_out, sem):
    copy = pltpu.make_async_copy(ig_in, ig_out, sem)
    copy.start()
    j = lax.axis_index("tm") * 2 + lax.axis_index("rows")
    for k in range(8):
        @pl.when(j == k)
        def _(k=k):
            wg_out[...] = fin[k:k + 81, :] * SCALE
    copy.wait()


def per_device(inputs, cotangent, weight, gain, shift_term):
    f32, bf16 = jnp.float32, jnp.bfloat16
    hbm = pl.BlockSpec(memory_space=pltpu.HBM)
    vmem = pl.BlockSpec(memory_space=pltpu.VMEM)
    dma = pltpu.SemaphoreType.DMA
    ig, fin = pl.pallas_call(
        kernel,
        out_shape=(pltpu.VMEM((OWN, C), bf16), pltpu.VMEM((88, C), f32)),
        in_specs=[hbm, hbm, hbm, vmem, vmem],
        out_specs=(vmem, vmem),
        scratch_shapes=[
            pltpu.VMEM((OWN, C), bf16),
            pltpu.VMEM((C, OWN), bf16),
            pltpu.VMEM((SL, 2 * POS), bf16),
            pltpu.VMEM((2, POS + OWN, C), bf16),
            pltpu.VMEM((27, SL, C), bf16),
            pltpu.VMEM((2, C, 128), f32),
            pltpu.VMEM((SL, 128), f32),
            pltpu.VMEM((SL, 2 * POS), f32),
            pltpu.VMEM((SL, 2 * POS), f32),
            pltpu.VMEM((864, POS), bf16),
            pltpu.VMEM((1296, C), f32),
            pltpu.VMEM((SL, 2 * POS), bf16),
            pltpu.VMEM((C, OWN), bf16),
            pltpu.VMEM((2, 6, MSG, C), bf16),
            pltpu.VMEM((2, 6, MSG, C), bf16),
            pltpu.VMEM((2, WIN1, C), f32),
            pltpu.VMEM((2, 3, WIN2, C), f32),
            pltpu.VMEM((2, WIN2, C), f32),
            dma((4 + NG,)), dma((NG, 10)), dma((NG, 10)), dma((7,)), dma((7,)), dma((7,)), dma((7,)),
            dma((NCH, 18)), dma((NCH, 18)), dma((NCH, 24)), dma((NCH,)),
        ],
        compiler_params=pltpu.CompilerParams(
            collective_id=0, has_side_effects=True, vmem_limit_bytes=56 * 1024 * 1024
        ),
        name="resblock_backward",
    )(
        inputs.reshape(OWN, C),
        cotangent.reshape(OWN, C),
        weight.reshape(27, C, C),
        gain,
        shift_term,
    )
    ig, fin = (pltpu.with_memory_space_constraint(v, pltpu.VMEM) for v in (ig, fin))
    ig, wg = pl.pallas_call(
        write_out,
        out_shape=(
            jax.ShapeDtypeStruct((OWN, C), bf16),
            jax.ShapeDtypeStruct((81, C), f32),
        ),
        in_specs=[vmem, vmem],
        out_specs=(hbm, vmem),
        scratch_shapes=[dma],
        name="write_out",
    )(ig, fin)
    return ig.reshape(1, 2, 1, 128, C), wg


def solution(mesh):
    return jax.shard_map(
        per_device,
        mesh=mesh,
        in_specs=(
            P("clip", "tm", "rows", None, None),
            P("clip", "tm", "rows", None, None),
            P(),
            P(),
            P(),
        ),
        out_specs=(P("clip", "tm", "rows", None, None), P(("clip", "tm", "rows"), None)),
        check_vma=False,
    )
```

time: 48.9 us -> 43.1 us (0.88)
  Pallas kernels: 48 us -> 42.3 us
    pallas_call x1, Pallas kernels: 46.6 us -> 41 us  [per_device(): pl.pallas_call(kernel, out_shape=(pltpu.VMEM((OWN, C), bf16), pltpu.VMEM(...]
where the time goes in v3:
time: 43.1 us; the launch traced here: 42.9 us
  Pallas kernels  42.3 us (98%)
  between operations  0.64 us (1%)
    pallas_call x1, Pallas kernels, per_device(): pl.pallas_call(kernel, out_shape=(pltpu.VMEM((OWN, C), bf16), pltpu.VMEM(...  41 us
    pallas_call x1, Pallas kernels, per_device(): pl.pallas_call(write_out, out_shape=(jax.ShapeDtypeStruct((OWN, C), bf16)...  1.34 us

profile of v3, /device:TPU:1, one launch (start us, length us, event | category | flops | bytes accessed | tf_op | source)
XLA Modules:
  0.0 42.9 jit_solution(16263613907655628520)
XLA Ops:
  0.6 41.0 %resblock_backward.1 = (bf16[256,384]{1,0:T(8,128)(2,1)S(1)}, f32[88,384]{1,0:T(8,128)S(1)}) custom-call(bf16[256,384]{1,0:T(8,128)(2,1)} %bitcast.7, bf16[256,384]{1,0:T(8,128)(2,1)} %bitcast.8, bf16[27,384,384]{2,1,0:T(8,128)(2,1)} %bitcast.6, f32[384]{0:T(512)} %gain_ref.1, f32[384]{0:T(512)} %shift_ref.1), custom_call_target="tpu_custom_call" | custom-call | tf_op jit(solution)/shard_map/resblock_backward/pallas_call | solution.py:520
  41.6 1.3 %write_out.1 = (bf16[256,384]{1,0:T(8,128)(2,1)}, f32[81,384]{1,0:T(8,128)}) custom-call(bf16[256,384]{1,0:T(8,128)(2,1)S(1)} %get-tuple-element.6.ig_in, f32[88,384]{1,0:T(8,128)S(1)} %get-tuple-element.7.fin), custom_call_target="tpu_custom_call" | custom-call | tf_op jit(solution)/shard_map/write_out/pallas_call | solution.py:559

commit v4 on v3

--- a/solution.py
+++ b/solution.py
@@ -26,16 +26,17 @@
 
 
 MSG = 96
+MSG2 = 64
 SPAN = 125.0
 
 
-def encode(values):
+def encode(values, size):
     n, w = values.shape
     tiles = values.reshape(n // 8, 8, w)
     top = jnp.max(jnp.abs(tiles), axis=0) * 1.01 + 1e-30
     top = top.astype(jnp.bfloat16).astype(jnp.float32)
     code = jnp.exp2(tiles * (SPAN / top)[None]).reshape(n, w)
-    return jnp.concatenate([code] + [top] * ((MSG - n) // 8), 0).astype(jnp.bfloat16)
+    return jnp.concatenate([code] + [top] * ((size - n) // 8), 0).astype(jnp.bfloat16)
 
 
 def decode(message, n):
@@ -47,8 +48,8 @@
 
 def kernel(
     x_hbm, cot_hbm, w_hbm, gain_ref, shift_ref, ig_ref, fin,
-    x_own, x_send, x_all, cot, wv, gb, stat, normed_s, dsil_s, lcat, part,
-    ig_send, ig_recv, out_b, in_b, res1, ebuf, res2,
+    x_own, x_send, x_all, cot, wv, gb, stat, normed_s, dsil_s, lcat, prod, part,
+    ig_send, ig_recv, out_b, in_b, res1, fout_b, fin_b, res2,
     loc_sem, cs_send, cs_recv, xs_send, xs_recv, is_send, is_recv, r_send, r_recv, f_send, f_recv,
 ):
     clip, tm, rows = lax.axis_index("clip"), lax.axis_index("tm"), lax.axis_index("rows")
@@ -134,6 +135,8 @@
         c_in[ch].wait()
         send(ch, 0, (rows, frame(tm, 0)), right)
         send(ch, 2, (rows, frame(tm, 1)), left)
+
+    def own_rest(ch):
         send(ch, 1, (rows, frame(tm, 1)), right)
         send(ch, 3, (rows, frame(tm, 0)), left)
         send(ch, 4, (rows, own_slot), sib)
@@ -155,10 +158,12 @@
         arrived(ch, 6, (orow, frame(ot, 1)))
         send(ch, 9, whole((ot, orow)), sib)
 
-    def gathered(ch):
+    def gathered_near(ch):
         arrived(ch, 4, sib_of((tm, rows)))
         arrived(ch, 7, sib_of((lt, lr)))
         arrived(ch, 8, sib_of((rt, rr)))
+
+    def gathered_far(ch):
         arrived(ch, 9, sib_of((ot, orow)))
 
     own(0)
@@ -182,6 +187,7 @@
     mine = pl.ds(pl.multiple_of(j * SL, SL), SL)
     gain_l, shift_l = gb[0, mine, :], gb[1, mine, :]
 
+    own_rest(0)
     fwd1(0)
 
     me = clip * 8 + j
@@ -265,17 +271,24 @@
                         r0 = h * 432 + (dt * 3 + dw) * SL
                         lcat[r0:r0 + SL, t_out * 128:(t_out + 1) * 128] = a
 
-    def weight_grad(ch):
-        lo, hi = CH[ch][0], sum(CH[ch])
-        r_0 = jnp.dot(lcat[...], cot[0, 0:POS, lo:hi], preferred_element_type=jnp.float32)
-        r_1 = jnp.dot(lcat[...], cot[1, 0:POS, lo:hi], preferred_element_type=jnp.float32)
+    half = POS // 2
+    near_k = pl.ds(pl.multiple_of(x_hi * half, half), half)
+    far_k = pl.ds(pl.multiple_of((1 - x_hi) * half, half), half)
+
+    def weight_grad_near():
+        prod[1 - rows] = jnp.dot(lcat[...], cot[1 - rows, 0:POS, :], preferred_element_type=jnp.float32)
+
+    def weight_grad_far():
+        prod[rows] = jnp.dot(lcat[:, near_k], cot[rows, near_k, :], preferred_element_type=jnp.float32)
+        gathered_far(0)
+        prod[rows] += jnp.dot(lcat[:, far_k], cot[rows, far_k, :], preferred_element_type=jnp.float32)
         for dt in range(3):
             for dw in range(3):
                 q = (dt * 3 + dw) * SL
-                near = [r[k:k + SL] for r in (r_0, r_1) for k in (q, q + 432)]
+                near = [prod[r, k:k + SL] for r in range(2) for k in (q, q + 432)]
                 for dh, v in ((0, near[2]), (1, near[0] + near[3]), (2, near[1])):
                     r0 = ORDER.index(dt * 9 + dh * 3 + dw) * SL
-                    part[r0:r0 + SL, lo:hi] = v
+                    part[r0:r0 + SL] = v
 
     def ring_copy(ch, slot, src, dst, to):
         return pltpu.make_async_remote_copy(
@@ -296,7 +309,7 @@
             ]
 
         def put(self, k, values):
-            self.out_b[k] = encode(values)
+            self.out_b[k] = encode(values, MSG)
             self.all[k].start()
 
         def got(self, k, n):
@@ -322,21 +335,22 @@
             )
 
     class Direct:
-        def __init__(self, ch, slot, src, pos, to, bufs, out):
-            self.src, self.bufs, self.out = src, bufs, out
+        def __init__(self, ch, slot, src, pos, to, out_b, in_b, out):
+            self.src, self.out_b, self.in_b, self.out = src, out_b, in_b, out
             self.at = [pl.ds(pl.multiple_of(((pos + k) % 4) * HOP2, 8), WIN2) for k in range(4)]
-            self.all = [
-                ring_copy(ch, slot + k - 1, src.at[self.at[k]], bufs.at[k - 1], to[k - 1]) for k in (2, 1, 3)
-            ]
+            self.all = [ring_copy(ch, slot + k, out_b.at[k], in_b.at[k], to[k]) for k in range(3)]
 
         def start(self):
-            for c in self.all:
-                c.start()
+            for k in (1, 0, 2):
+                self.out_b[k] = encode(self.src[self.at[k + 1], :], MSG2)
+                self.all[k].start()
 
         def end(self):
-            for c in self.all:
-                c.wait_recv()
-            self.out[...] = self.src[self.at[0], :] + self.bufs[0] + self.bufs[1] + self.bufs[2]
+            total = self.src[self.at[0], :]
+            for k in (0, 2, 1):
+                self.all[k].wait_recv()
+                total = total + decode(self.in_b[k], WIN2)
+            self.out[...] = total
 
     first, second = [], []
     for c in range(NCH):
@@ -351,7 +365,7 @@
             ))
             second.append(Direct(
                 c, 12 + a * 3, res1.at[a, :, lanes], pos2, (plus2, far2, minus2),
-                ebuf.at[a, :, :, lanes], res2.at[a, :, lanes],
+                fout_b.at[a, :, :, lanes], fin_b.at[a, :, :, lanes], res2.at[a, :, lanes],
             ))
 
     def start1(ch):
@@ -372,9 +386,9 @@
             nxt.start()
 
     def end2(ch):
-        for st in second[2 * ch:2 * ch + 2]:
-            st.end()
-        scatter(ch, begin)
+        for a in range(2):
+            second[2 * ch + a].end()
+            scatter(ch, begin, a * 12, a * 12 + 12)
 
     nt = (((1,), (1,)), ((), ()))
     grads, cots = [], []
@@ -440,8 +454,9 @@
             c.wait_recv()
         ig_ref[...] = ig_recv[...].astype(jnp.float32).T.astype(jnp.bfloat16)
 
-    def scatter(ch, act):
-        for n, (ok, d_to, slot) in enumerate(jobs):
+    def scatter(ch, act, lo=0, hi=24):
+        for n in range(lo, hi):
+            ok, d_to, slot = jobs[n]
             src = res2.at[n // 12, pl.ds(n % 6 * 8, 8), pl.ds(*CH[ch])]
             act(ch, n, ok, src, d_to, slot)
 
@@ -469,9 +484,10 @@
             fin_copy(ch, n, src, d_to, slot).wait_send()
 
     fwd2(0)
+    gathered_near(0)
+    weight_grad_near()
     fwd3(0)
-    gathered(0)
-    weight_grad(0)
+    weight_grad_far()
     start1(0)
     near1(0)
     w_in.wait()
@@ -533,13 +549,15 @@
             pltpu.VMEM((SL, 2 * POS), f32),
             pltpu.VMEM((SL, 2 * POS), f32),
             pltpu.VMEM((864, POS), bf16),
+            pltpu.VMEM((2, 864, C), f32),
             pltpu.VMEM((1296, C), f32),
             pltpu.VMEM((SL, 2 * POS), bf16),
             pltpu.VMEM((C, OWN), bf16),
             pltpu.VMEM((2, 6, MSG, C), bf16),
             pltpu.VMEM((2, 6, MSG, C), bf16),
             pltpu.VMEM((2, WIN1, C), f32),
-            pltpu.VMEM((2, 3, WIN2, C), f32),
+            pltpu.VMEM((2, 3, MSG2, C), bf16),
+            pltpu.VMEM((2, 3, MSG2, C), bf16),
             pltpu.VMEM((2, WIN2, C), f32),
             dma((4 + NG,)), dma((NG, 10)), dma((NG, 10)), dma((7,)), dma((7,)), dma((7,)), dma((7,)),
             dma((NCH, 18)), dma((NCH, 18)), dma((NCH, 24)), dma((NCH,)),

time: 43.1 us -> 40.8 us (0.947)
  Pallas kernels: 42.3 us -> 40 us
    pallas_call x1, Pallas kernels: 41 us -> 38.7 us  [per_device(): pl.pallas_call(kernel, out_shape=(pltpu.VMEM((OWN, C), bf16), pltpu.VMEM(...]
where the time goes in v4:
time: 40.8 us; the launch traced here: 40.6 us
  Pallas kernels  40 us (98%)
  between operations  0.64 us (2%)
    pallas_call x1, Pallas kernels, per_device(): pl.pallas_call(kernel, out_shape=(pltpu.VMEM((OWN, C), bf16), pltpu.VMEM(...  38.7 us
    pallas_call x1, Pallas kernels, per_device(): pl.pallas_call(write_out, out_shape=(jax.ShapeDtypeStruct((OWN, C), bf16)...  1.34 us

profile of v4, /device:TPU:1, one launch (start us, length us, event | category | flops | bytes accessed | tf_op | source)
XLA Modules:
  0.0 40.6 jit_solution(7229310872535657619)
XLA Ops:
  0.6 38.7 %resblock_backward.1 = (bf16[256,384]{1,0:T(8,128)(2,1)S(1)}, f32[88,384]{1,0:T(8,128)S(1)}) custom-call(bf16[256,384]{1,0:T(8,128)(2,1)} %bitcast.7, bf16[256,384]{1,0:T(8,128)(2,1)} %bitcast.8, bf16[27,384,384]{2,1,0:T(8,128)(2,1)} %bitcast.6, f32[384]{0:T(512)} %gain_ref.1, f32[384]{0:T(512)} %shift_ref.1), custom_call_target="tpu_custom_call" | custom-call | tf_op jit(solution)/shard_map/resblock_backward/pallas_call | solution.py:536
  39.3 1.3 %write_out.1 = (bf16[256,384]{1,0:T(8,128)(2,1)}, f32[81,384]{1,0:T(8,128)}) custom-call(bf16[256,384]{1,0:T(8,128)(2,1)S(1)} %get-tuple-element.6.ig_in, f32[88,384]{1,0:T(8,128)S(1)} %get-tuple-element.7.fin), custom_call_target="tpu_custom_call" | custom-call | tf_op jit(solution)/shard_map/write_out/pallas_call | solution.py:577

commit v5 on v4

--- a/solution.py
+++ b/solution.py
@@ -70,6 +70,17 @@
     ot, orow = ring(tm, rows, 2)
     sib_tm = x_hi * 2 + (1 - core)
 
+    yp, ym = ((yy + 1) % 4) * 4 + zz, ((yy + 3) % 4) * 4 + zz
+    yo, zo = ((yy + 2) % 4) * 4 + zz, yy * 4 + (zz + 2) % 4
+    zp, zm = yy * 4 + (zz + 1) % 4, yy * 4 + (zz + 3) % 4
+    barrier = pltpu.get_barrier_semaphore()
+    for k in range(1, 8):
+        p = (j + k) % 8
+        pl.semaphore_signal(barrier, inc=1, device_id=dev(p // 2, p % 2), device_id_type=MESH)
+    for other in (yp, ym, zp, zm):
+        pl.semaphore_signal(barrier, inc=1, device_id=(other, tm, rows), device_id_type=MESH)
+
+
     x_in = pltpu.make_async_copy(x_hbm, x_own, loc_sem.at[0])
     x_in.start()
     own_slot = pl.ds(pl.multiple_of(tm * OWN, OWN), OWN)
@@ -85,22 +96,6 @@
     )
     w_in.start()
 
-    yp, ym = ((yy + 1) % 4) * 4 + zz, ((yy + 3) % 4) * 4 + zz
-    yo, zo = ((yy + 2) % 4) * 4 + zz, yy * 4 + (zz + 2) % 4
-    zp, zm = yy * 4 + (zz + 1) % 4, yy * 4 + (zz + 3) % 4
-    barrier = pltpu.get_barrier_semaphore()
-    for k in range(1, 8):
-        p = (j + k) % 8
-        pl.semaphore_signal(barrier, inc=1, device_id=dev(p // 2, p % 2), device_id_type=MESH)
-    for other in (yp, ym, zp, zm):
-        pl.semaphore_signal(barrier, inc=1, device_id=(other, tm, rows), device_id_type=MESH)
-
-    x_in.wait()
-    x_send[...] = x_own[...].astype(jnp.float32).T.astype(jnp.bfloat16)
-    gb[0] = jnp.broadcast_to(gain_ref[...].reshape(1, C), (128, C)).T
-    gb[1] = jnp.broadcast_to(shift_ref[...].reshape(1, C), (128, C)).T
-    for h in range(2):
-        cot[h, POS:, :] = jnp.zeros((OWN, C), jnp.bfloat16)
     pl.semaphore_wait(barrier, 11)
 
     def frame(tm_, f):
@@ -168,6 +163,8 @@
 
     own(0)
 
+    x_in.wait()
+    x_send[...] = x_own[...].astype(jnp.float32).T.astype(jnp.bfloat16)
     own_lanes = pl.ds(pl.multiple_of(rows * POS + tm * OWN, OWN), OWN)
     x_self = pltpu.make_async_copy(
         x_send.at[pl.ds(pl.multiple_of(j * SL, SL), SL)], x_all.at[:, own_lanes], loc_sem.at[3]
@@ -184,10 +181,15 @@
         c.start()
         xs.append(c)
 
+    own_rest(0)
+
+    gb[0] = jnp.broadcast_to(gain_ref[...].reshape(1, C), (128, C)).T
+    gb[1] = jnp.broadcast_to(shift_ref[...].reshape(1, C), (128, C)).T
+    for h in range(2):
+        cot[h, POS:, :] = jnp.zeros((OWN, C), jnp.bfloat16)
     mine = pl.ds(pl.multiple_of(j * SL, SL), SL)
     gain_l, shift_l = gb[0, mine, :], gb[1, mine, :]
 
-    own_rest(0)
     fwd1(0)
 
     me = clip * 8 + j
@@ -502,8 +504,8 @@
     for c in [ig_self] + igs:
         c.start()
     turn(0)
+    end2(0)
     ig_out()
-    end2(0)
 
     for c in sends + xs + igs:
         c.wait_send()

time: 40.8 us -> 40.8 us (level)
  no operation moved by 1% of the time
where the time goes in v5:
time: 40.8 us; the launch traced here: 40.6 us
  Pallas kernels  40 us (98%)
  between operations  0.64 us (2%)
    pallas_call x1, Pallas kernels, per_device(): pl.pallas_call(kernel, out_shape=(pltpu.VMEM((OWN, C), bf16), pltpu.VMEM(...  38.7 us
    pallas_call x1, Pallas kernels, per_device(): pl.pallas_call(write_out, out_shape=(jax.ShapeDtypeStruct((OWN, C), bf16)...  1.34 us

profile of v5, /device:TPU:1, one launch (start us, length us, event | category | flops | bytes accessed | tf_op | source)
XLA Modules:
  0.0 40.6 jit_solution(15826949555294151711)
XLA Ops:
  0.6 38.7 %resblock_backward.1 = (bf16[256,384]{1,0:T(8,128)(2,1)S(1)}, f32[88,384]{1,0:T(8,128)S(1)}) custom-call(bf16[256,384]{1,0:T(8,128)(2,1)} %bitcast.7, bf16[256,384]{1,0:T(8,128)(2,1)} %bitcast.8, bf16[27,384,384]{2,1,0:T(8,128)(2,1)} %bitcast.6, f32[384]{0:T(512)} %gain_ref.1, f32[384]{0:T(512)} %shift_ref.1), custom_call_target="tpu_custom_call" | custom-call | tf_op jit(solution)/shard_map/resblock_backward/pallas_call | solution.py:538
  39.3 1.3 %write_out.1 = (bf16[256,384]{1,0:T(8,128)(2,1)}, f32[81,384]{1,0:T(8,128)}) custom-call(bf16[256,384]{1,0:T(8,128)(2,1)S(1)} %get-tuple-element.6.ig_in, f32[88,384]{1,0:T(8,128)S(1)} %get-tuple-element.7.fin), custom_call_target="tpu_custom_call" | custom-call | tf_op jit(solution)/shard_map/write_out/pallas_call | solution.py:579

commit v6 on v5

--- a/solution.py
+++ b/solution.py
@@ -513,10 +513,10 @@
         for c in st.all:
             c.wait_send()
     for c in range(NCH):
+        scatter(c, finish)
+    for c in range(NCH):
         lanes = fin.at[:, pl.ds(*CH[c])]
         pltpu.make_async_copy(lanes, lanes, f_recv.at[c]).wait()
-    for c in range(NCH):
-        scatter(c, finish)
 
 
 def write_out(ig_in, fin, ig_out, wg_out, sem):

time: 40.8 us -> 40.8 us (level)
  no operation moved by 1% of the time
where the time goes in v6:
time: 40.8 us; the launch traced here: 40.6 us
  Pallas kernels  40 us (98%)
  between operations  0.64 us (2%)
    pallas_call x1, Pallas kernels, per_device(): pl.pallas_call(kernel, out_shape=(pltpu.VMEM((OWN, C), bf16), pltpu.VMEM(...  38.6 us
    pallas_call x1, Pallas kernels, per_device(): pl.pallas_call(write_out, out_shape=(jax.ShapeDtypeStruct((OWN, C), bf16)...  1.34 us

profile of v6, /device:TPU:1, one launch (start us, length us, event | category | flops | bytes accessed | tf_op | source)
XLA Modules:
  0.0 40.6 jit_solution(6527044480619206863)
XLA Ops:
  0.6 38.6 %resblock_backward.1 = (bf16[256,384]{1,0:T(8,128)(2,1)S(1)}, f32[88,384]{1,0:T(8,128)S(1)}) custom-call(bf16[256,384]{1,0:T(8,128)(2,1)} %bitcast.7, bf16[256,384]{1,0:T(8,128)(2,1)} %bitcast.8, bf16[27,384,384]{2,1,0:T(8,128)(2,1)} %bitcast.6, f32[384]{0:T(512)} %gain_ref.1, f32[384]{0:T(512)} %shift_ref.1), custom_call_target="tpu_custom_call" | custom-call | tf_op jit(solution)/shard_map/resblock_backward/pallas_call | solution.py:538
  39.3 1.3 %write_out.1 = (bf16[256,384]{1,0:T(8,128)(2,1)}, f32[81,384]{1,0:T(8,128)}) custom-call(bf16[256,384]{1,0:T(8,128)(2,1)S(1)} %get-tuple-element.6.ig_in, f32[88,384]{1,0:T(8,128)S(1)} %get-tuple-element.7.fin), custom_call_target="tpu_custom_call" | custom-call | tf_op jit(solution)/shard_map/write_out/pallas_call | solution.py:579
